TPU v7x, 512 devices: a whole 4x4x16 slice. The times are simulated.
512 devices in a mesh: tm: 128 (over x, z, core), space: 4 (over y).
Axes of the slice: x: 4, y: 4, z: 16, core: 2. Of those that a mesh axis runs over, the one named last changes fastest.
Arguments:
- forcing: float32 [2048, 64, 2048], P('tm', 'space'), may hold values from -4 to 4
- iterate: float32 [512, 64, 2048], P('tm', 'space'), may hold values from -6 to 6
- permeability: float32 [64, 2048], P('space'), may hold values from 0.5 to 1
Outputs:
- updated: float32 [512, 64, 2048], P('tm', 'space')
All inputs are finite; a program needn't handle non-finite values.
Results may differ from a plain program's by a relative error of at most 0.00002.
Values sent between devices are 32-bit elements; how exact they have to be, the bound alone decides.
A program may use at most 64 MiB of HBM per device.

v0:
```python
import jax
import jax.numpy as jnp
from jax import lax
from jax.sharding import PartitionSpec as P

SWEEPS = 6


step_scale = 0.06


def extended_2(x, sides, width):
    for axis, dim in sides:
        size, length = (lax.axis_size(axis), x.shape[dim])
        up = [(i, (i + 1) % size) for i in range(size - 1)]
        down = [(j, i) for i, j in up]
        last = lax.slice_in_dim(x, length - width, length, axis=dim)
        first = lax.slice_in_dim(x, 0, width, axis=dim)
        before = lax.ppermute(last, axis, up)
        after = lax.ppermute(first, axis, down)
        x = jnp.concatenate([before, x, after], axis=dim)
    return x


def shifted(x, axis, by):
    length = lax.axis_size(axis)
    pairs = [(i, i + by) for i in range(length) if 0 <= i + by < length]
    return lax.ppermute(x, axis, pairs)


def stepper(field, coeff, factor):
    padded = jnp.pad(field, [(0, 0)] * (field.ndim - 1) + [(1, 1)])
    kpad = jnp.pad(coeff, ((0, 0), (1, 1)))
    center = padded[..., 1:-1, 1:-1]
    kmid = kpad[1:-1, 1:-1]
    flux = jnp.zeros_like(center)
    for rshift, cshift in ((1, 0), (-1, 0), (0, 1), (0, -1)):
        knext = kpad[
            1 + rshift : kpad.shape[0] - 1 + rshift, 1 + cshift : kpad.shape[1] - 1 + cshift
        ]
        vnext = padded[
            ...,
            1 + rshift : padded.shape[-2] - 1 + rshift,
            1 + cshift : padded.shape[-1] - 1 + cshift,
        ]
        flux = flux + 0.5 * (kmid + knext) * (vnext - center)
    return center + factor * flux


def per_device(forcing, iterate, permeability):
    rows = iterate.shape[1]
    cols = iterate.shape[2]
    c_mid = 4.0 * step_scale
    c_top = 4.0 * step_scale
    krim = extended_2(permeability, (("space", 0),), 5)

    def kslice(depth):
        return krim[5 - depth : 5 + rows + depth]

    def mid_step(field, factor):
        extended = extended_2(field, (("space", 0),), 1)
        return stepper(extended, kslice(1), factor)

    blocks = forcing.reshape(4, 4, rows, cols)

    def fine_step(field):
        padded = extended_2(field, (("space", 1),), 1)
        return stepper(padded, kslice(1), step_scale)

    state = iterate
    for section in range(1, 4):
        state = fine_step(state) + blocks[:, section]
    ahead = fine_step(state)
    previous = shifted(ahead[3], "tm", 1)
    before = jnp.concatenate([previous[None], ahead[:3]], axis=0)
    resid = blocks[:, 0] + before - iterate
    level = resid[1]
    level = mid_step(level, c_mid) + resid[2]
    level = mid_step(level, c_mid) + resid[3]
    onward = mid_step(level, c_mid)
    coarse_src = resid[0] + shifted(onward, "tm", 1)
    coarse = coarse_src
    for sweep in range(SWEEPS):
        behind = shifted(coarse, "tm", 1)
        coarse = coarse_src + mid_step(behind, c_top)
    first = mid_step(coarse, c_mid) + resid[1]
    second = mid_step(first, c_mid) + resid[2]
    third = mid_step(second, c_mid) + resid[3]
    return iterate + jnp.stack([coarse, first, second, third], axis=0)


def solution(mesh):
    in_specs = (P("tm", "space", None), P("tm", "space", None), P("space", None))
    out_specs = P("tm", "space", None)
    return jax.shard_map(
        per_device, mesh=mesh, in_specs=in_specs, out_specs=out_specs, check_vma=False
    )
```

profile of v0, /device:TPU:6, one launch (start us, length us, event | category | flops | bytes accessed | tf_op | source)
XLA Modules:
  0.0 209.9 jit_solution(16299812400562958081)
XLA Ops:
  1.2 3.5 %collective-permute-start.3 = (f32[4,1,2048]{2,1,0:T(1,128)S(1)}, f32[4,1,2048]{2,1,0:T(1,128)S(1)}, u32[]{:S(2)}, u32[]{:S(2)}) collective-permute-start(f32[4,1,2048]{2,1,0:T(1,128)S(1)} %get-tuple-element.13), channel_id=1, source_target_pairs={{0,1},{1,2},{2,3},{4,5},{5,6},{6,7},{8,9},{9,10},{10,11},{12,13},{... | collective-permute-start | bytes 98312 | tf_op jit(solution)/shard_map/ppermute | solution.py:19
  6.9 4.5 %collective-permute-start.2 = (f32[5,2048]{1,0:T(8,128)S(1)}, f32[5,2048]{1,0:T(8,128)S(1)}, u32[]{:S(2)}, u32[]{:S(2)}) collective-permute-start(f32[5,2048]{1,0:T(8,128)S(1)} %get-tuple-element.43), channel_id=1, source_target_pairs={{0,1},{1,2},{2,3},{4,5},{5,6},{6,7},{8,9},{9,10},{10,11},{12,13},{... | collective-permute-start | bytes 122888 | tf_op jit(solution)/shard_map/ppermute | solution.py:19
  14.3 3.3 %collective-permute-done = f32[5,2048]{1,0:T(8,128)S(1)} collective-permute-done((f32[5,2048]{1,0:T(8,128)S(1)}, f32[5,2048]{1,0:T(8,128)S(1)}, u32[]{:S(2)}, u32[]{:S(2)}) %collective-permute-start) | collective-permute-done | bytes 40992 | tf_op jit(solution)/shard_map/ppermute | solution.py:20
  19.4 3.5 %collective-permute-start.5 = (f32[4,1,2048]{2,1,0:T(1,128)S(1)}, f32[4,1,2048]{2,1,0:T(1,128)S(1)}, u32[]{:S(2)}, u32[]{:S(2)}) collective-permute-start(f32[4,1,2048]{2,1,0:T(1,128)S(1)} %get-tuple-element.11), channel_id=1, source_target_pairs={{0,1},{1,2},{2,3},{4,5},{5,6},{6,7},{8,9},{9,10},{10,11},{12,13},{... | collective-permute-start | bytes 98312 | tf_op jit(solution)/shard_map/ppermute | solution.py:19
  24.4 4.2 %collective-permute-done.4 = f32[4,1,2048]{2,1,0:T(1,128)S(1)} collective-permute-done((f32[4,1,2048]{2,1,0:T(1,128)S(1)}, f32[4,1,2048]{2,1,0:T(1,128)S(1)}, u32[]{:S(2)}, u32[]{:S(2)}) %collective-permute-start.4) | collective-permute-done | bytes 32800 | tf_op jit(solution)/shard_map/ppermute | solution.py:20
  29.6 3.2 %collective-permute-start.7 = (f32[4,1,2048]{2,1,0:T(1,128)S(1)}, f32[4,1,2048]{2,1,0:T(1,128)S(1)}, u32[]{:S(2)}, u32[]{:S(2)}) collective-permute-start(f32[4,1,2048]{2,1,0:T(1,128)S(1)} %get-tuple-element.9), channel_id=1, source_target_pairs={{0,1},{1,2},{2,3},{4,5},{5,6},{6,7},{8,9},{9,10},{10,11},{12,13},{... | collective-permute-start | bytes 98312 | tf_op jit(solution)/shard_map/ppermute | solution.py:19
  34.4 4.2 %collective-permute-done.6 = f32[4,1,2048]{2,1,0:T(1,128)S(1)} collective-permute-done((f32[4,1,2048]{2,1,0:T(1,128)S(1)}, f32[4,1,2048]{2,1,0:T(1,128)S(1)}, u32[]{:S(2)}, u32[]{:S(2)}) %collective-permute-start.6) | collective-permute-done | bytes 32800 | tf_op jit(solution)/shard_map/ppermute | solution.py:20
  43.1 4.2 %collective-permute-done.8 = f32[4,1,2048]{2,1,0:T(1,128)S(1)} collective-permute-done((f32[4,1,2048]{2,1,0:T(1,128)S(1)}, f32[4,1,2048]{2,1,0:T(1,128)S(1)}, u32[]{:S(2)}, u32[]{:S(2)}) %collective-permute-start.8) | collective-permute-done | bytes 32800 | tf_op jit(solution)/shard_map/ppermute | solution.py:20
  48.2 1.9 collective-permute-start.10
  50.2 6.4 %collective-permute-done.10 = f32[16,2048]{1,0:T(8,128)S(1)} collective-permute-done((f32[16,2048]{1,0:T(8,128)S(1)}, f32[16,2048]{1,0:T(8,128)S(1)}, u32[]{:S(2)}, u32[]{:S(2)}) %collective-permute-start.10) | collective-permute-done | bytes 131104 | tf_op jit(solution)/shard_map/ppermute | solution.py:28
  60.0 4.2 %collective-permute-done.11 = f32[1,2048]{1,0:T(1,128)S(1)} collective-permute-done((f32[1,2048]{1,0:T(1,128)S(1)}, f32[1,2048]{1,0:T(1,128)S(1)}, u32[]{:S(2)}, u32[]{:S(2)}) %collective-permute-start.11) | collective-permute-done | bytes 8224 | tf_op jit(solution)/shard_map/ppermute | solution.py:20
  67.8 4.2 %collective-permute-done.13 = f32[1,2048]{1,0:T(1,128)S(1)} collective-permute-done((f32[1,2048]{1,0:T(1,128)S(1)}, f32[1,2048]{1,0:T(1,128)S(1)}, u32[]{:S(2)}, u32[]{:S(2)}) %collective-permute-start.13) | collective-permute-done | bytes 8224 | tf_op jit(solution)/shard_map/ppermute | solution.py:20
  75.6 4.2 %collective-permute-done.15 = f32[1,2048]{1,0:T(1,128)S(1)} collective-permute-done((f32[1,2048]{1,0:T(1,128)S(1)}, f32[1,2048]{1,0:T(1,128)S(1)}, u32[]{:S(2)}, u32[]{:S(2)}) %collective-permute-start.15) | collective-permute-done | bytes 8224 | tf_op jit(solution)/shard_map/ppermute | solution.py:20
  82.0 6.5 %collective-permute-done.17 = f32[16,2048]{1,0:T(8,128)S(1)} collective-permute-done((f32[16,2048]{1,0:T(8,128)S(1)}, f32[16,2048]{1,0:T(8,128)S(1)}, u32[]{:S(2)}, u32[]{:S(2)}) %collective-permute-start.17) | collective-permute-done | bytes 131104 | tf_op jit(solution)/shard_map/ppermute | solution.py:28
  90.4 6.5 %collective-permute-done.18 = f32[16,2048]{1,0:T(8,128)S(1)} collective-permute-done((f32[16,2048]{1,0:T(8,128)S(1)}, f32[16,2048]{1,0:T(8,128)S(1)}, u32[]{:S(2)}, u32[]{:S(2)}) %collective-permute-start.18) | collective-permute-done | bytes 131104 | tf_op jit(solution)/shard_map/ppermute | solution.py:28
  96.9 1.9 collective-permute-start.20
  100.2 4.2 %collective-permute-done.19 = f32[1,2048]{1,0:T(1,128)S(1)} collective-permute-done((f32[1,2048]{1,0:T(1,128)S(1)}, f32[1,2048]{1,0:T(1,128)S(1)}, u32[]{:S(2)}, u32[]{:S(2)}) %collective-permute-start.19) | collective-permute-done | bytes 8224 | tf_op jit(solution)/shard_map/ppermute | solution.py:20
  106.6 6.5 %collective-permute-done.21 = f32[16,2048]{1,0:T(8,128)S(1)} collective-permute-done((f32[16,2048]{1,0:T(8,128)S(1)}, f32[16,2048]{1,0:T(8,128)S(1)}, u32[]{:S(2)}, u32[]{:S(2)}) %collective-permute-start.21) | collective-permute-done | bytes 131104 | tf_op jit(solution)/shard_map/ppermute | solution.py:28
  113.1 1.9 collective-permute-start.23
  116.4 4.2 %collective-permute-done.22 = f32[1,2048]{1,0:T(1,128)S(1)} collective-permute-done((f32[1,2048]{1,0:T(1,128)S(1)}, f32[1,2048]{1,0:T(1,128)S(1)}, u32[]{:S(2)}, u32[]{:S(2)}) %collective-permute-start.22) | collective-permute-done | bytes 8224 | tf_op jit(solution)/shard_map/ppermute | solution.py:20
  122.8 6.5 %collective-permute-done.24 = f32[16,2048]{1,0:T(8,128)S(1)} collective-permute-done((f32[16,2048]{1,0:T(8,128)S(1)}, f32[16,2048]{1,0:T(8,128)S(1)}, u32[]{:S(2)}, u32[]{:S(2)}) %collective-permute-start.24) | collective-permute-done | bytes 131104 | tf_op jit(solution)/shard_map/ppermute | solution.py:28
  132.6 4.2 %collective-permute-done.25 = f32[1,2048]{1,0:T(1,128)S(1)} collective-permute-done((f32[1,2048]{1,0:T(1,128)S(1)}, f32[1,2048]{1,0:T(1,128)S(1)}, u32[]{:S(2)}, u32[]{:S(2)}) %collective-permute-start.25) | collective-permute-done | bytes 8224 | tf_op jit(solution)/shard_map/ppermute | solution.py:20
  139.0 6.5 %collective-permute-done.27 = f32[16,2048]{1,0:T(8,128)S(1)} collective-permute-done((f32[16,2048]{1,0:T(8,128)S(1)}, f32[16,2048]{1,0:T(8,128)S(1)}, u32[]{:S(2)}, u32[]{:S(2)}) %collective-permute-start.27) | collective-permute-done | bytes 131104 | tf_op jit(solution)/shard_map/ppermute | solution.py:28
  148.7 4.2 %collective-permute-done.28 = f32[1,2048]{1,0:T(1,128)S(1)} collective-permute-done((f32[1,2048]{1,0:T(1,128)S(1)}, f32[1,2048]{1,0:T(1,128)S(1)}, u32[]{:S(2)}, u32[]{:S(2)}) %collective-permute-start.28) | collective-permute-done | bytes 8224 | tf_op jit(solution)/shard_map/ppermute | solution.py:20
  155.2 6.5 %collective-permute-done.30 = f32[16,2048]{1,0:T(8,128)S(1)} collective-permute-done((f32[16,2048]{1,0:T(8,128)S(1)}, f32[16,2048]{1,0:T(8,128)S(1)}, u32[]{:S(2)}, u32[]{:S(2)}) %collective-permute-start.30) | collective-permute-done | bytes 131104 | tf_op jit(solution)/shard_map/ppermute | solution.py:28
  164.9 4.2 %collective-permute-done.31 = f32[1,2048]{1,0:T(1,128)S(1)} collective-permute-done((f32[1,2048]{1,0:T(1,128)S(1)}, f32[1,2048]{1,0:T(1,128)S(1)}, u32[]{:S(2)}, u32[]{:S(2)}) %collective-permute-start.31) | collective-permute-done | bytes 8224 | tf_op jit(solution)/shard_map/ppermute | solution.py:20
  171.4 6.5 %collective-permute-done.33 = f32[16,2048]{1,0:T(8,128)S(1)} collective-permute-done((f32[16,2048]{1,0:T(8,128)S(1)}, f32[16,2048]{1,0:T(8,128)S(1)}, u32[]{:S(2)}, u32[]{:S(2)}) %collective-permute-start.33) | collective-permute-done | bytes 131104 | tf_op jit(solution)/shard_map/ppermute | solution.py:28
  181.1 4.2 %collective-permute-done.34 = f32[1,2048]{1,0:T(1,128)S(1)} collective-permute-done((f32[1,2048]{1,0:T(1,128)S(1)}, f32[1,2048]{1,0:T(1,128)S(1)}, u32[]{:S(2)}, u32[]{:S(2)}) %collective-permute-start.34) | collective-permute-done | bytes 8224 | tf_op jit(solution)/shard_map/ppermute | solution.py:20
  188.9 4.2 %collective-permute-done.36 = f32[1,2048]{1,0:T(1,128)S(1)} collective-permute-done((f32[1,2048]{1,0:T(1,128)S(1)}, f32[1,2048]{1,0:T(1,128)S(1)}, u32[]{:S(2)}, u32[]{:S(2)}) %collective-permute-start.36) | collective-permute-done | bytes 8224 | tf_op jit(solution)/shard_map/ppermute | solution.py:20
  193.4 1.9 collective-permute-start.39
  196.7 4.2 %collective-permute-done.38 = f32[1,2048]{1,0:T(1,128)S(1)} collective-permute-done((f32[1,2048]{1,0:T(1,128)S(1)}, f32[1,2048]{1,0:T(1,128)S(1)}, u32[]{:S(2)}, u32[]{:S(2)}) %collective-permute-start.38) | collective-permute-done | bytes 8224 | tf_op jit(solution)/shard_map/ppermute | solution.py:20
  204.5 4.2 %collective-permute-done.40 = f32[1,2048]{1,0:T(1,128)S(1)} collective-permute-done((f32[1,2048]{1,0:T(1,128)S(1)}, f32[1,2048]{1,0:T(1,128)S(1)}, u32[]{:S(2)}, u32[]{:S(2)}) %collective-permute-start.40) | collective-permute-done | bytes 8224 | tf_op jit(solution)/shard_map/ppermute | solution.py:20
  (115 shorter events, 68.7 us)
Async XLA Ops:
  1.2 11.5 %collective-permute-start.3 = (f32[4,1,2048]{2,1,0:T(1,128)S(1)}, f32[4,1,2048]{2,1,0:T(1,128)S(1)}, u32[]{:S(2)}, u32[]{:S(2)}) collective-permute-start(f32[4,1,2048]{2,1,0:T(1,128)S(1)} %get-tuple-element.13), channel_id=1, source_target_pairs={{0,1},{1,2},{2,3},{4,5},{5,6},{6,7},{8,9},{9,10},{10,11},{12,13},{... | collective-permute-start | bytes 98312 | tf_op jit(solution)/shard_map/ppermute | solution.py:19
  4.7 8.1 %collective-permute-start.1 = (f32[4,1,2048]{2,1,0:T(1,128)S(1)}, f32[4,1,2048]{2,1,0:T(1,128)S(1)}, u32[]{:S(2)}, u32[]{:S(2)}) collective-permute-start(f32[4,1,2048]{2,1,0:T(1,128)S(1)} %get-tuple-element.14), channel_id=1, source_target_pairs={{1,0},{2,1},{3,2},{5,4},{6,5},{7,6},{9,8},{10,9},{11,10},{13,12},{... | collective-permute-start | bytes 98312 | tf_op jit(solution)/shard_map/ppermute | solution.py:20
  6.9 7.4 %collective-permute-start.2 = (f32[5,2048]{1,0:T(8,128)S(1)}, f32[5,2048]{1,0:T(8,128)S(1)}, u32[]{:S(2)}, u32[]{:S(2)}) collective-permute-start(f32[5,2048]{1,0:T(8,128)S(1)} %get-tuple-element.43), channel_id=1, source_target_pairs={{0,1},{1,2},{2,3},{4,5},{5,6},{6,7},{8,9},{9,10},{10,11},{12,13},{... | collective-permute-start | bytes 122888 | tf_op jit(solution)/shard_map/ppermute | solution.py:19
  11.5 6.2 %collective-permute-start = (f32[5,2048]{1,0:T(8,128)S(1)}, f32[5,2048]{1,0:T(8,128)S(1)}, u32[]{:S(2)}, u32[]{:S(2)}) collective-permute-start(f32[5,2048]{1,0:T(8,128)S(1)} %get-tuple-element.44), channel_id=1, source_target_pairs={{1,0},{2,1},{3,2},{5,4},{6,5},{7,6},{9,8},{10,9},{11,10},{13,12},{... | collective-permute-start | bytes 122888 | tf_op jit(solution)/shard_map/ppermute | solution.py:20
  19.4 5.1 %collective-permute-start.5 = (f32[4,1,2048]{2,1,0:T(1,128)S(1)}, f32[4,1,2048]{2,1,0:T(1,128)S(1)}, u32[]{:S(2)}, u32[]{:S(2)}) collective-permute-start(f32[4,1,2048]{2,1,0:T(1,128)S(1)} %get-tuple-element.11), channel_id=1, source_target_pairs={{0,1},{1,2},{2,3},{4,5},{5,6},{6,7},{8,9},{9,10},{10,11},{12,13},{... | collective-permute-start | bytes 98312 | tf_op jit(solution)/shard_map/ppermute | solution.py:19
  22.9 5.8 %collective-permute-start.4 = (f32[4,1,2048]{2,1,0:T(1,128)S(1)}, f32[4,1,2048]{2,1,0:T(1,128)S(1)}, u32[]{:S(2)}, u32[]{:S(2)}) collective-permute-start(f32[4,1,2048]{2,1,0:T(1,128)S(1)} %get-tuple-element.12), channel_id=1, source_target_pairs={{1,0},{2,1},{3,2},{5,4},{6,5},{7,6},{9,8},{10,9},{11,10},{13,12},{... | collective-permute-start | bytes 98312 | tf_op jit(solution)/shard_map/ppermute | solution.py:20
  29.6 4.8 %collective-permute-start.7 = (f32[4,1,2048]{2,1,0:T(1,128)S(1)}, f32[4,1,2048]{2,1,0:T(1,128)S(1)}, u32[]{:S(2)}, u32[]{:S(2)}) collective-permute-start(f32[4,1,2048]{2,1,0:T(1,128)S(1)} %get-tuple-element.9), channel_id=1, source_target_pairs={{0,1},{1,2},{2,3},{4,5},{5,6},{6,7},{8,9},{9,10},{10,11},{12,13},{... | collective-permute-start | bytes 98312 | tf_op jit(solution)/shard_map/ppermute | solution.py:19
  32.8 5.8 %collective-permute-start.6 = (f32[4,1,2048]{2,1,0:T(1,128)S(1)}, f32[4,1,2048]{2,1,0:T(1,128)S(1)}, u32[]{:S(2)}, u32[]{:S(2)}) collective-permute-start(f32[4,1,2048]{2,1,0:T(1,128)S(1)} %get-tuple-element.10), channel_id=1, source_target_pairs={{1,0},{2,1},{3,2},{5,4},{6,5},{7,6},{9,8},{10,9},{11,10},{13,12},{... | collective-permute-start | bytes 98312 | tf_op jit(solution)/shard_map/ppermute | solution.py:20
  39.6 3.5 %collective-permute-start.9 = (f32[4,1,2048]{2,1,0:T(1,128)S(1)}, f32[4,1,2048]{2,1,0:T(1,128)S(1)}, u32[]{:S(2)}, u32[]{:S(2)}) collective-permute-start(f32[4,1,2048]{2,1,0:T(1,128)S(1)} %get-tuple-element.7), channel_id=1, source_target_pairs={{0,1},{1,2},{2,3},{4,5},{5,6},{6,7},{8,9},{9,10},{10,11},{12,13},{... | collective-permute-start | bytes 98312 | tf_op jit(solution)/shard_map/ppermute | solution.py:19
  41.5 5.8 %collective-permute-start.8 = (f32[4,1,2048]{2,1,0:T(1,128)S(1)}, f32[4,1,2048]{2,1,0:T(1,128)S(1)}, u32[]{:S(2)}, u32[]{:S(2)}) collective-permute-start(f32[4,1,2048]{2,1,0:T(1,128)S(1)} %get-tuple-element.8), channel_id=1, source_target_pairs={{1,0},{2,1},{3,2},{5,4},{6,5},{7,6},{9,8},{10,9},{11,10},{13,12},{... | collective-permute-start | bytes 98312 | tf_op jit(solution)/shard_map/ppermute | solution.py:20
  48.2 8.4 %collective-permute-start.10 = (f32[16,2048]{1,0:T(8,128)S(1)}, f32[16,2048]{1,0:T(8,128)S(1)}, u32[]{:S(2)}, u32[]{:S(2)}) collective-permute-start(f32[16,2048]{1,0:T(8,128)S(1)} %slice_bitcast_fusion.8), channel_id=1, source_target_pairs={{0,4},{4,8},{8,12},{12,16},{16,20},{20,24},{24,28},{28,32},{32,36}... | collective-permute-start | bytes 393224 | tf_op jit(solution)/shard_map/ppermute | solution.py:28
  58.7 5.5 %collective-permute-start.11 = (f32[1,2048]{1,0:T(1,128)S(1)}, f32[1,2048]{1,0:T(1,128)S(1)}, u32[]{:S(2)}, u32[]{:S(2)}) collective-permute-start(f32[1,2048]{1,0:T(1,128)S(1)} %get-tuple-element.6), channel_id=1, source_target_pairs={{1,0},{2,1},{3,2},{5,4},{6,5},{7,6},{9,8},{10,9},{11,10},{13,12},{... | collective-permute-start | bytes 24584 | tf_op jit(solution)/shard_map/ppermute | solution.py:20
  66.5 5.5 %collective-permute-start.13 = (f32[1,2048]{1,0:T(1,128)S(1)}, f32[1,2048]{1,0:T(1,128)S(1)}, u32[]{:S(2)}, u32[]{:S(2)}) collective-permute-start(f32[1,2048]{1,0:T(1,128)S(1)} %get-tuple-element.38), channel_id=1, source_target_pairs={{1,0},{2,1},{3,2},{5,4},{6,5},{7,6},{9,8},{10,9},{11,10},{13,12},{... | collective-permute-start | bytes 24584 | tf_op jit(solution)/shard_map/ppermute | solution.py:20
  74.2 5.5 %collective-permute-start.15 = (f32[1,2048]{1,0:T(1,128)S(1)}, f32[1,2048]{1,0:T(1,128)S(1)}, u32[]{:S(2)}, u32[]{:S(2)}) collective-permute-start(f32[1,2048]{1,0:T(1,128)S(1)} %get-tuple-element.36), channel_id=1, source_target_pairs={{1,0},{2,1},{3,2},{5,4},{6,5},{7,6},{9,8},{10,9},{11,10},{13,12},{... | collective-permute-start | bytes 24584 | tf_op jit(solution)/shard_map/ppermute | solution.py:20
  80.1 8.4 %collective-permute-start.17 = (f32[16,2048]{1,0:T(8,128)S(1)}, f32[16,2048]{1,0:T(8,128)S(1)}, u32[]{:S(2)}, u32[]{:S(2)}) collective-permute-start(f32[16,2048]{1,0:T(8,128)S(1)} %fusion.163), channel_id=1, source_target_pairs={{0,4},{4,8},{8,12},{12,16},{16,20},{20,24},{24,28},{28,32},{32,36}... | collective-permute-start | bytes 393224 | tf_op jit(solution)/shard_map/ppermute | solution.py:28
  88.5 8.4 %collective-permute-start.18 = (f32[16,2048]{1,0:T(8,128)S(1)}, f32[16,2048]{1,0:T(8,128)S(1)}, u32[]{:S(2)}, u32[]{:S(2)}) collective-permute-start(f32[16,2048]{1,0:T(8,128)S(1)} %fusion.195), channel_id=1, source_target_pairs={{0,4},{4,8},{8,12},{12,16},{16,20},{20,24},{24,28},{28,32},{32,36}... | collective-permute-start | bytes 393224 | tf_op jit(solution)/shard_map/ppermute | solution.py:28
  96.9 3.3 %collective-permute-start.20 = (f32[1,2048]{1,0:T(1,128)S(1)}, f32[1,2048]{1,0:T(1,128)S(1)}, u32[]{:S(2)}, u32[]{:S(2)}) collective-permute-start(f32[1,2048]{1,0:T(1,128)S(1)} %get-tuple-element.33), channel_id=1, source_target_pairs={{0,1},{1,2},{2,3},{4,5},{5,6},{6,7},{8,9},{9,10},{10,11},{12,13},{... | collective-permute-start | bytes 24584 | tf_op jit(solution)/shard_map/ppermute | solution.py:19
  98.8 5.5 %collective-permute-start.19 = (f32[1,2048]{1,0:T(1,128)S(1)}, f32[1,2048]{1,0:T(1,128)S(1)}, u32[]{:S(2)}, u32[]{:S(2)}) collective-permute-start(f32[1,2048]{1,0:T(1,128)S(1)} %get-tuple-element.34), channel_id=1, source_target_pairs={{1,0},{2,1},{3,2},{5,4},{6,5},{7,6},{9,8},{10,9},{11,10},{13,12},{... | collective-permute-start | bytes 24584 | tf_op jit(solution)/shard_map/ppermute | solution.py:20
  104.7 8.4 %collective-permute-start.21 = (f32[16,2048]{1,0:T(8,128)S(1)}, f32[16,2048]{1,0:T(8,128)S(1)}, u32[]{:S(2)}, u32[]{:S(2)}) collective-permute-start(f32[16,2048]{1,0:T(8,128)S(1)} %fusion.152), channel_id=1, source_target_pairs={{0,4},{4,8},{8,12},{12,16},{16,20},{20,24},{24,28},{28,32},{32,36}... | collective-permute-start | bytes 393224 | tf_op jit(solution)/shard_map/ppermute | solution.py:28
  115.0 5.5 %collective-permute-start.22 = (f32[1,2048]{1,0:T(1,128)S(1)}, f32[1,2048]{1,0:T(1,128)S(1)}, u32[]{:S(2)}, u32[]{:S(2)}) collective-permute-start(f32[1,2048]{1,0:T(1,128)S(1)} %get-tuple-element.32), channel_id=1, source_target_pairs={{1,0},{2,1},{3,2},{5,4},{6,5},{7,6},{9,8},{10,9},{11,10},{13,12},{... | collective-permute-start | bytes 24584 | tf_op jit(solution)/shard_map/ppermute | solution.py:20
  120.9 8.4 %collective-permute-start.24 = (f32[16,2048]{1,0:T(8,128)S(1)}, f32[16,2048]{1,0:T(8,128)S(1)}, u32[]{:S(2)}, u32[]{:S(2)}) collective-permute-start(f32[16,2048]{1,0:T(8,128)S(1)} %fusion.140), channel_id=1, source_target_pairs={{0,4},{4,8},{8,12},{12,16},{16,20},{20,24},{24,28},{28,32},{32,36}... | collective-permute-start | bytes 393224 | tf_op jit(solution)/shard_map/ppermute | solution.py:28
  131.2 5.5 %collective-permute-start.25 = (f32[1,2048]{1,0:T(1,128)S(1)}, f32[1,2048]{1,0:T(1,128)S(1)}, u32[]{:S(2)}, u32[]{:S(2)}) collective-permute-start(f32[1,2048]{1,0:T(1,128)S(1)} %get-tuple-element.30), channel_id=1, source_target_pairs={{1,0},{2,1},{3,2},{5,4},{6,5},{7,6},{9,8},{10,9},{11,10},{13,12},{... | collective-permute-start | bytes 24584 | tf_op jit(solution)/shard_map/ppermute | solution.py:20
  137.1 8.4 %collective-permute-start.27 = (f32[16,2048]{1,0:T(8,128)S(1)}, f32[16,2048]{1,0:T(8,128)S(1)}, u32[]{:S(2)}, u32[]{:S(2)}) collective-permute-start(f32[16,2048]{1,0:T(8,128)S(1)} %fusion.128), channel_id=1, source_target_pairs={{0,4},{4,8},{8,12},{12,16},{16,20},{20,24},{24,28},{28,32},{32,36}... | collective-permute-start | bytes 393224 | tf_op jit(solution)/shard_map/ppermute | solution.py:28
  147.4 5.5 %collective-permute-start.28 = (f32[1,2048]{1,0:T(1,128)S(1)}, f32[1,2048]{1,0:T(1,128)S(1)}, u32[]{:S(2)}, u32[]{:S(2)}) collective-permute-start(f32[1,2048]{1,0:T(1,128)S(1)} %get-tuple-element.28), channel_id=1, source_target_pairs={{1,0},{2,1},{3,2},{5,4},{6,5},{7,6},{9,8},{10,9},{11,10},{13,12},{... | collective-permute-start | bytes 24584 | tf_op jit(solution)/shard_map/ppermute | solution.py:20
  153.2 8.4 %collective-permute-start.30 = (f32[16,2048]{1,0:T(8,128)S(1)}, f32[16,2048]{1,0:T(8,128)S(1)}, u32[]{:S(2)}, u32[]{:S(2)}) collective-permute-start(f32[16,2048]{1,0:T(8,128)S(1)} %fusion.116), channel_id=1, source_target_pairs={{0,4},{4,8},{8,12},{12,16},{16,20},{20,24},{24,28},{28,32},{32,36}... | collective-permute-start | bytes 393224 | tf_op jit(solution)/shard_map/ppermute | solution.py:28
  163.6 5.5 %collective-permute-start.31 = (f32[1,2048]{1,0:T(1,128)S(1)}, f32[1,2048]{1,0:T(1,128)S(1)}, u32[]{:S(2)}, u32[]{:S(2)}) collective-permute-start(f32[1,2048]{1,0:T(1,128)S(1)} %get-tuple-element.26), channel_id=1, source_target_pairs={{1,0},{2,1},{3,2},{5,4},{6,5},{7,6},{9,8},{10,9},{11,10},{13,12},{... | collective-permute-start | bytes 24584 | tf_op jit(solution)/shard_map/ppermute | solution.py:20
  169.4 8.4 %collective-permute-start.33 = (f32[16,2048]{1,0:T(8,128)S(1)}, f32[16,2048]{1,0:T(8,128)S(1)}, u32[]{:S(2)}, u32[]{:S(2)}) collective-permute-start(f32[16,2048]{1,0:T(8,128)S(1)} %fusion.104), channel_id=1, source_target_pairs={{0,4},{4,8},{8,12},{12,16},{16,20},{20,24},{24,28},{28,32},{32,36}... | collective-permute-start | bytes 393224 | tf_op jit(solution)/shard_map/ppermute | solution.py:28
  179.8 5.5 %collective-permute-start.34 = (f32[1,2048]{1,0:T(1,128)S(1)}, f32[1,2048]{1,0:T(1,128)S(1)}, u32[]{:S(2)}, u32[]{:S(2)}) collective-permute-start(f32[1,2048]{1,0:T(1,128)S(1)} %get-tuple-element.24), channel_id=1, source_target_pairs={{1,0},{2,1},{3,2},{5,4},{6,5},{7,6},{9,8},{10,9},{11,10},{13,12},{... | collective-permute-start | bytes 24584 | tf_op jit(solution)/shard_map/ppermute | solution.py:20
  187.6 5.5 %collective-permute-start.36 = (f32[1,2048]{1,0:T(1,128)S(1)}, f32[1,2048]{1,0:T(1,128)S(1)}, u32[]{:S(2)}, u32[]{:S(2)}) collective-permute-start(f32[1,2048]{1,0:T(1,128)S(1)} %get-tuple-element.22), channel_id=1, source_target_pairs={{1,0},{2,1},{3,2},{5,4},{6,5},{7,6},{9,8},{10,9},{11,10},{13,12},{... | collective-permute-start | bytes 24584 | tf_op jit(solution)/shard_map/ppermute | solution.py:20
  193.4 3.3 %collective-permute-start.39 = (f32[1,2048]{1,0:T(1,128)S(1)}, f32[1,2048]{1,0:T(1,128)S(1)}, u32[]{:S(2)}, u32[]{:S(2)}) collective-permute-start(f32[1,2048]{1,0:T(1,128)S(1)} %get-tuple-element.19), channel_id=1, source_target_pairs={{0,1},{1,2},{2,3},{4,5},{5,6},{6,7},{8,9},{9,10},{10,11},{12,13},{... | collective-permute-start | bytes 24584 | tf_op jit(solution)/shard_map/ppermute | solution.py:19
  195.4 5.5 %collective-permute-start.38 = (f32[1,2048]{1,0:T(1,128)S(1)}, f32[1,2048]{1,0:T(1,128)S(1)}, u32[]{:S(2)}, u32[]{:S(2)}) collective-permute-start(f32[1,2048]{1,0:T(1,128)S(1)} %get-tuple-element.20), channel_id=1, source_target_pairs={{1,0},{2,1},{3,2},{5,4},{6,5},{7,6},{9,8},{10,9},{11,10},{13,12},{... | collective-permute-start | bytes 24584 | tf_op jit(solution)/shard_map/ppermute | solution.py:20
  203.2 5.5 %collective-permute-start.40 = (f32[1,2048]{1,0:T(1,128)S(1)}, f32[1,2048]{1,0:T(1,128)S(1)}, u32[]{:S(2)}, u32[]{:S(2)}) collective-permute-start(f32[1,2048]{1,0:T(1,128)S(1)} %get-tuple-element.18), channel_id=1, source_target_pairs={{1,0},{2,1},{3,2},{5,4},{6,5},{7,6},{9,8},{10,9},{11,10},{13,12},{... | collective-permute-start | bytes 24584 | tf_op jit(solution)/shard_map/ppermute | solution.py:20
  (13 other events, 89.1 us)
where the time goes:
time: 211 us; the launch traced here: 210 us
  waiting for transfers between devices  120 us (57%)
  starting transfers between devices  77 us (36%)
  other arithmetic  10.2 us (5%)
  local copies, waits for them, and re-layouts  2.48 us (1%)
    ppermute x17, waiting for transfers between devices, extended_2(): after = lax.ppermute(first, axis, down)  66.4 us
    ppermute x8, waiting for transfers between devices, shifted(): return lax.ppermute(x, axis, pairs)  51.7 us
    ppermute x17, starting transfers between devices, extended_2(): before = lax.ppermute(last, axis, up)  39.7 us
    ppermute x17, starting transfers between devices, extended_2(): after = lax.ppermute(first, axis, down)  22 us
    ppermute x8, starting transfers between devices, shifted(): return lax.ppermute(x, axis, pairs)  15.4 us
    concatenate x17, other arithmetic, extended_2(): x = jnp.concatenate([before, x, after], axis=dim)  5.67 us
  transfers between devices with their start and end apart: 42, of which 27 were waited for; matrix products, arithmetic and copies ran while one was open for 1% of the time, Pallas kernels for 0%

commit v1 on v0

v1 whole, which is shorter than its diff:
```python
import jax
import jax.numpy as jnp
from jax import lax
from jax.experimental import pallas as pl
from jax.experimental.pallas import tpu as pltpu
from jax.sharding import PartitionSpec as P

STEP = 0.06
NT = 128
NS = 4
ROWS = 16
EXT = 24
COLS = 2048
WIDTH = 512
MESH = pl.DeviceIdType.MESH
NCOPY = 112


def strips(body):
    def one(j, carry):
        body(pl.multiple_of(j * WIDTH, 128))
        return carry

    lax.fori_loop(0, COLS // WIDTH, one, 0)


def stencil(load, weights, at, rows):
    v = load(at, WIDTH)
    left = load(pl.multiple_of(lax.rem(at + COLS - 128, COLS), 128), 128)
    right = load(pl.multiple_of(lax.rem(at + WIDTH, COLS), 128), 128)
    wide = WIDTH + 128
    vl = pltpu.roll(jnp.concatenate([left[:rows], v[:rows]], axis=1), 1, axis=1)[:, 128:]
    vr = pltpu.roll(jnp.concatenate([v[:rows], right[:rows]], axis=1), wide - 1, axis=1)[:, :WIDTH]
    above = pltpu.roll(v, 1, axis=0)[:rows]
    below = pltpu.roll(v, EXT - 1, axis=0)[:rows]

    def w(i):
        return weights[i, 0:rows, pl.ds(at, WIDTH)]

    return w(0) * v[:rows] + w(1) * above + w(2) * below + (w(3) * vl + w(4) * vr)


def plain(ref, rows=EXT):
    return lambda at, width: ref[0:rows, pl.ds(at, width)]


def kernel(
    forcing, iterate, perm, out,
    f_buf, i_buf, k_buf, w_fine, w_mid, a_buf, ahead, r_buf, b_buf, g_buf, pg, ppg, ge_in,
    u_buf, u_in, y_buf, yc, m1, m1_in, q_buf, tmp, m2, m2_in, x_buf, e_buf, base, o_buf,
    send, recv, local, out_sem,
):
    t = lax.axis_index("tm")
    s = lax.axis_index("space")
    core = lax.rem(t, 2)
    chip = t // 2
    up = lax.rem(s + NS - 1, NS)
    down = lax.rem(s + 1, NS)
    mate = t + 1 - 2 * core
    count = [0]

    def shift(by):
        return lax.rem(t + by + NT, NT)

    def remote(src, dst, tm, sp):
        i = count[0]
        count[0] += 1
        return pltpu.make_async_remote_copy(
            src_ref=src, dst_ref=dst, send_sem=send.at[i], recv_sem=recv.at[i],
            device_id=(tm, sp), device_id_type=MESH,
        )

    def edges(src, dst, tm, depth):
        return [
            remote(src.at[0:depth], dst.at[ROWS : ROWS + depth], tm, up),
            remote(src.at[ROWS - depth : ROWS], dst.at[EXT - depth : EXT], tm, down),
        ]

    def start(copies):
        for c in copies:
            c.start()

    def arrive(copies):
        for c in copies:
            c.wait_recv()

    def sent(copies):
        for c in copies:
            c.wait_send()

    loads = [pltpu.make_async_copy(perm, k_buf.at[0:ROWS], local.at[0])]
    for p in range(4):
        loads.append(pltpu.make_async_copy(iterate.at[p], i_buf.at[p, 0:ROWS], local.at[1 + p]))
        loads.append(
            pltpu.make_async_copy(
                forcing.at[4 * p : 4 * p + 4], f_buf.at[4 * p : 4 * p + 4, 0:ROWS], local.at[5 + p]
            )
        )
    for c in loads:
        c.start()

    barrier = pltpu.get_barrier_semaphore()

    def greet(tm, sp):
        pl.semaphore_signal(barrier, inc=1, device_id=(tm, sp), device_id_type=MESH)

    greet(t, up)
    greet(t, down)
    greet(mate, s)
    for by in (-2, -4):
        for sp in (s, up, down):
            greet(shift(by), sp)

    @pl.when(core == 0)
    def _():
        for sp in (s, up, down):
            greet(shift(-3), sp)

    @pl.when(core == 1)
    def _():
        greet(shift(-3), s)
        for sp in (up, down):
            greet(mate, sp)

    pl.semaphore_wait(barrier, 12)

    k_halo = edges(perm, k_buf, t, 4)
    start(k_halo)
    halo = []
    for p in range(4):
        one = edges(iterate.at[p], i_buf.at[p], t, 4)
        for j in (1, 2, 3):
            one += edges(forcing.at[4 * p + j], f_buf.at[4 * p + j], t, 4 - j)
        if p == 0:
            one += edges(forcing.at[0], f_buf.at[0], t, 3)
        start(one)
        halo.append(one)

    for c in loads:
        c.wait()
    arrive(k_halo)

    row = lax.broadcasted_iota(jnp.int32, (EXT, 128), 0)
    is_below = jnp.logical_and(row >= ROWS, row < ROWS + 4)
    is_above = row >= ROWS + 4
    outside = jnp.logical_or(
        jnp.logical_and(is_below, s == NS - 1), jnp.logical_and(is_above, s == 0)
    )
    inside = jnp.where(outside, 0.0, 1.0).astype(jnp.float32)
    lane = lax.broadcasted_iota(jnp.int32, (EXT, 128), 1)

    def weigh(j, carry):
        at = pl.multiple_of(j * 128, 128)
        last = COLS // 128 - 1
        k = k_buf[:, pl.ds(at, 128)] * inside
        kl = k_buf[:, pl.ds(pl.multiple_of(lax.rem(at + COLS - 128, COLS), 128), 128)] * inside
        kr = k_buf[:, pl.ds(pl.multiple_of(lax.rem(at + 128, COLS), 128), 128)] * inside
        first_lane = jnp.logical_and(lane == 0, j == 0)
        last_lane = jnp.logical_and(lane == 127, j == last)
        k_left = jnp.where(lane == 0, pltpu.roll(kl, 1, axis=1), pltpu.roll(k, 1, axis=1))
        k_right = jnp.where(lane == 127, pltpu.roll(kr, 127, axis=1), pltpu.roll(k, 127, axis=1))
        k_left = jnp.where(first_lane, 0.0, k_left)
        k_right = jnp.where(last_lane, 0.0, k_right)
        k_above = pltpu.roll(k, 1, axis=0)
        k_below = pltpu.roll(k, EXT - 1, axis=0)
        in_above = pltpu.roll(inside, 1, axis=0) * inside
        in_below = pltpu.roll(inside, EXT - 1, axis=0) * inside
        wa = 0.5 * (k + k_above)
        wb = 0.5 * (k + k_below)
        wl = 0.5 * (k + k_left)
        wr = 0.5 * (k + k_right)
        total = (wa + wb) + (wl + wr)
        for ref, c in ((w_fine, STEP), (w_mid, 4.0 * STEP)):
            ref[0, :, pl.ds(at, 128)] = 1.0 - c * total
            ref[1, :, pl.ds(at, 128)] = c * (wa * in_above)
            ref[2, :, pl.ds(at, 128)] = c * (wb * in_below)
            ref[3, :, pl.ds(at, 128)] = jnp.where(first_lane, 0.0, c * wl)
            ref[4, :, pl.ds(at, 128)] = jnp.where(last_lane, 0.0, c * wr)
        return carry

    lax.fori_loop(0, COLS // 128, weigh, 0)

    def run(src, weights, rows, finish):
        def body(at):
            finish(at, pl.ds(at, WIDTH), stencil(plain(src), weights, at, rows))

        strips(body)

    def store(dst, rows):
        def finish(at, cols, value):
            dst[0:rows, cols] = value

        return finish

    r_halo = {}
    early = []
    early_mate = []
    for p in range(4):
        arrive(halo[p])
        state = i_buf.at[p]
        for j in (1, 2, 3):
            nxt = a_buf.at[p, j - 1]

            def finish(at, cols, value, nxt=nxt, j=j, p=p):
                nxt[:, cols] = value + f_buf[4 * p + j, :, cols]

            run(state, w_fine, EXT, finish)
            state = nxt
        if p < 3:

            def finish(at, cols, value, p=p):
                r_buf[p, 0:ROWS, cols] = (
                    f_buf[4 * p + 4, 0:ROWS, cols] + value - i_buf[p + 1, 0:ROWS, cols]
                )

            run(state, w_fine, ROWS, finish)
            r_halo[p] = edges(r_buf.at[p], r_buf.at[p], t, 3 - p)
            start(r_halo[p])
        else:
            run(state, w_fine, ROWS, store(ahead, ROWS))
        if p == 0:

            def make_g(at):
                cols = pl.ds(at, WIDTH)
                g_buf[:, cols] = f_buf[0, :, cols] - i_buf[0, :, cols]

            strips(make_g)
            early = [remote(g_buf, ge_in, shift(3), s)]
            early_mate = [remote(ppg, ppg, mate, s)]

            @pl.when(core == 0)
            def _():
                start(early)

            run(g_buf, w_mid, EXT, store(pg, EXT))

            @pl.when(core == 0)
            def _():
                run(pg, w_mid, ROWS, store(ppg, ROWS))
                start(early_mate)

    arrive(r_halo[0])
    arrive(r_halo[1])

    def finish_b2(at, cols, value):
        b_buf[0, :, cols] = value + r_buf[1, :, cols]

    run(r_buf.at[0], w_mid, EXT, finish_b2)
    arrive(r_halo[2])

    def finish_b3(at, cols, value):
        b_buf[1, :, cols] = value + r_buf[2, :, cols]

    run(b_buf.at[0], w_mid, EXT, finish_b3)

    def finish_u(at, cols, value):
        u = value + ahead[0:ROWS, cols]
        u_buf[:, cols] = u
        y_buf[core, 0:ROWS, cols] = u + pg[0:ROWS, cols]

    run(b_buf.at[1], w_mid, ROWS, finish_u)

    y_main = [remote(y_buf.at[core, 0:ROWS], y_buf.at[core, 0:ROWS], mate, s)]
    y_edges = edges(y_buf.at[0], y_buf.at[0], t, 1)
    y_cross = edges(y_buf.at[0], y_buf.at[0], mate, 1)
    u_far = edges(u_buf, u_in, shift(3), 4) + [remote(u_buf, u_in.at[0:ROWS], shift(3), s)]

    @pl.when(core == 0)
    def _():
        start(y_edges)
        start(y_cross)

    start(y_main)

    @pl.when(core == 1)
    def _():
        start(u_far)

    def make_base(at):
        cols = pl.ds(at, WIDTH)
        base[0, :, cols] = i_buf[1, 0:ROWS, cols] + r_buf[0, 0:ROWS, cols]
        base[1, :, cols] = i_buf[2, 0:ROWS, cols] + b_buf[0, 0:ROWS, cols]
        base[2, :, cols] = i_buf[3, 0:ROWS, cols] + b_buf[1, 0:ROWS, cols]

    strips(make_base)

    @pl.when(core == 1)
    def _():
        arrive(early)
        arrive(early_mate)
        arrive(y_cross)

    @pl.when(core == 0)
    def _():
        arrive(y_edges)

    arrive(y_main)
    odd = core.astype(jnp.float32)

    def finish_m1(at, cols, value):
        both = value + y_buf[1, 0:ROWS, cols]
        yc[:, cols] = both
        m1[:, cols] = both - odd * ppg[:, cols]

    run(y_buf.at[0], w_mid, ROWS, finish_m1)
    m1_copies = edges(m1, m1_in, shift(2), 2) + [remote(m1, m1_in.at[0:ROWS], shift(2), s)]
    start(m1_copies)

    one = jnp.where(chip >= 1, 1.0, 0.0).astype(jnp.float32)
    two = jnp.where(chip >= 2, 1.0, 0.0).astype(jnp.float32)

    @pl.when(core == 0)
    def _():
        arrive(u_far)
        run(u_in, w_mid, EXT, store(tmp.at[0], EXT))

        def finish_q(at, cols, value):
            q_buf[:, cols] = two * value

        run(tmp.at[0], w_mid, EXT, finish_q)

    @pl.when(core == 1)
    def _():
        q_buf[...] = jnp.zeros_like(q_buf)

    arrive(m1_copies)

    def masked_m1(at, width):
        cols = pl.ds(at, width)
        return one * m1_in[:, cols] + q_buf[:, cols]

    def body_t3(at):
        tmp[1, :, pl.ds(at, WIDTH)] = stencil(masked_m1, w_mid, at, EXT)

    strips(body_t3)

    def finish_m2(at, cols, value):
        m2[:, cols] = value + yc[:, cols]

    run(tmp.at[1], w_mid, ROWS, finish_m2)
    m2_copies = edges(m2, m2_in, shift(4), 3) + [remote(m2, m2_in.at[0:ROWS], shift(4), s)]
    start(m2_copies)
    arrive(m2_copies)

    @pl.when(core == 0)
    def _():
        run(m2_in, w_mid, EXT, store(tmp.at[2], EXT))

        def finish_x(at, cols, value):
            x = g_buf[0:ROWS, cols] + one * m1_in[0:ROWS, cols] + two * value
            x_buf[0:ROWS, cols] = x
            o_buf[0, :, cols] = i_buf[0, 0:ROWS, cols] + x

        run(tmp.at[2], w_mid, ROWS, finish_x)

    @pl.when(core == 1)
    def _():
        def masked_m2(at, width):
            cols = pl.ds(at, width)
            return two * m2_in[:, cols] + one * ge_in[:, cols]

        def body(at):
            tmp[2, :, pl.ds(at, WIDTH)] = stencil(masked_m2, w_mid, at, EXT)

        strips(body)

        def finish_w(at, cols, value):
            tmp[3, :, cols] = value + one * m1_in[:, cols]

        run(tmp.at[2], w_mid, EXT, finish_w)

        def finish_x(at, cols, value):
            x = g_buf[0:ROWS, cols] + y_buf[0, 0:ROWS, cols] + value
            x_buf[0:ROWS, cols] = x
            o_buf[0, :, cols] = i_buf[0, 0:ROWS, cols] + x

        run(tmp.at[3], w_mid, ROWS, finish_x)

    x_copies = edges(x_buf, x_buf, t, 3)
    start(x_copies)
    outs = [pltpu.make_async_copy(o_buf.at[j], out.at[j], out_sem.at[j]) for j in range(4)]
    outs[0].start()
    arrive(x_copies)

    state = x_buf
    for j in (1, 2, 3):
        rows = EXT if j < 3 else ROWS

        def finish_e(at, cols, value, j=j):
            if j < 3:
                e_buf[j - 1, :, cols] = value
            o_buf[j, :, cols] = base[j - 1, :, cols] + value[:ROWS]

        run(state, w_mid, rows, finish_e)
        outs[j].start()
        if j < 3:
            state = e_buf.at[j - 1]

    for c in outs:
        c.wait()
    sent(k_halo)
    for p in range(4):
        sent(halo[p])
        if p < 3:
            sent(r_halo[p])
    sent(y_main)
    sent(m1_copies)
    sent(m2_copies)
    sent(x_copies)

    @pl.when(core == 0)
    def _():
        sent(early)
        sent(early_mate)
        sent(y_edges)
        sent(y_cross)

    @pl.when(core == 1)
    def _():
        sent(u_far)


def per_device(forcing, iterate, permeability):
    def field(*lead, rows=EXT):
        return pltpu.VMEM((*lead, rows, COLS), jnp.float32)

    scratch = [
        field(16),
        field(4),
        field(),
        field(5),
        field(5),
        field(4, 3),
        field(rows=ROWS),
        field(3),
        field(2),
        field(),
        field(),
        field(rows=ROWS),
        field(),
        field(rows=ROWS),
        field(),
        field(2),
        field(rows=ROWS),
        field(rows=ROWS),
        field(),
        field(),
        field(4),
        field(rows=ROWS),
        field(),
        field(),
        field(2),
        field(3, rows=ROWS),
        field(4, rows=ROWS),
        pltpu.SemaphoreType.DMA((NCOPY,)),
        pltpu.SemaphoreType.DMA((NCOPY,)),
        pltpu.SemaphoreType.DMA((9,)),
        pltpu.SemaphoreType.DMA((4,)),
    ]
    return pl.pallas_call(
        kernel,
        name="vcycle",
        out_shape=jax.ShapeDtypeStruct(iterate.shape, iterate.dtype),
        in_specs=[pl.BlockSpec(memory_space=pl.ANY)] * 3,
        out_specs=pl.BlockSpec(memory_space=pl.ANY),
        scratch_shapes=scratch,
        compiler_params=pltpu.CompilerParams(
            collective_id=0, has_side_effects=True, vmem_limit_bytes=40 * 2**20
        ),
    )(forcing, iterate, permeability)


def solution(mesh):
    in_specs = (P("tm", "space", None), P("tm", "space", None), P("space", None))
    out_specs = P("tm", "space", None)
    return jax.shard_map(
        per_device, mesh=mesh, in_specs=in_specs, out_specs=out_specs, check_vma=False
    )
```

time: 211 us -> 64.9 us (0.31)
  the two profiles are of different devices: /device:TPU:6 before, /device:TPU:1 now
where the time goes in v1:
time: 64.9 us; the launch traced here: 64.7 us
  Pallas kernels  60.3 us (93%)
  local copies, waits for them, and re-layouts  4.33 us (7%)
    pallas_call x1, Pallas kernels, per_device(): pl.pallas_call(kernel, name='vcycle', out_shape=jax.ShapeDtypeStruct(iter...  60.3 us
    unnamed x7, local copies, waits for them, and re-layouts  4.33 us

profile of v1, /device:TPU:1, one launch (start us, length us, event | category | flops | bytes accessed | tf_op | source)
XLA Modules:
  0.0 64.7 jit_solution(1723310979500447306)
XLA Ops:
  0.0 0.0 copy-start
  0.0 1.6 %copy-done = f32[16,16,2048]{2,1,0:T(8,128)S(1)} copy-done((f32[16,16,2048]{2,1,0:T(8,128)S(1)}, f32[16,16,2048]{2,1,0:T(8,128)}, u32[]{:S(2)}) %copy-start) | copy-done | bytes 2097176
  1.6 0.0 copy-start.1
  1.6 1.0 %copy-done.1 = f32[4,16,2048]{2,1,0:T(8,128)S(1)} copy-done((f32[4,16,2048]{2,1,0:T(8,128)S(1)}, f32[4,16,2048]{2,1,0:T(8,128)}, u32[]{:S(2)}) %copy-start.1) | copy-done | bytes 524312
  2.6 0.0 copy-start.2
  2.6 0.9 %copy-done.2 = f32[16,2048]{1,0:T(8,128)S(1)} copy-done((f32[16,2048]{1,0:T(8,128)S(1)}, f32[16,2048]{1,0:T(8,128)}, u32[]{:S(2)}) %copy-start.2) | copy-done | bytes 131096
  3.5 60.3 %vcycle.1 = f32[4,16,2048]{2,1,0:T(8,128)S(1)} custom-call(f32[16,16,2048]{2,1,0:T(8,128)S(1)} %copy-done, f32[4,16,2048]{2,1,0:T(8,128)S(1)} %copy-done.1, f32[16,2048]{1,0:T(8,128)S(1)} %copy-done.2), custom_call_target="tpu_custom_call" | custom-call | tf_op jit(solution)/shard_map/vcycle/pallas_call | solution.py:460
  63.9 0.8 %copy.5 = f32[4,16,2048]{2,1,0:T(8,128)} copy(f32[4,16,2048]{2,1,0:T(8,128)S(1)} %vcycle.1) | data formatting | bytes 1048576
Async XLA Ops:
  0.0 1.6 %copy-start = (f32[16,16,2048]{2,1,0:T(8,128)S(1)}, f32[16,16,2048]{2,1,0:T(8,128)}, u32[]{:S(2)}) copy-start(f32[16,16,2048]{2,1,0:T(8,128)} %forcing.1) | copy-start | bytes 6291460
  1.6 1.0 %copy-start.1 = (f32[4,16,2048]{2,1,0:T(8,128)S(1)}, f32[4,16,2048]{2,1,0:T(8,128)}, u32[]{:S(2)}) copy-start(f32[4,16,2048]{2,1,0:T(8,128)} %iterate.1) | copy-start | bytes 1572868
  2.6 0.9 %copy-start.2 = (f32[16,2048]{1,0:T(8,128)S(1)}, f32[16,2048]{1,0:T(8,128)}, u32[]{:S(2)}) copy-start(f32[16,2048]{1,0:T(8,128)} %perm.1) | copy-start | bytes 393220

commit v2 on v1

v2 whole, which is shorter than its diff:
```python
import jax
import jax.numpy as jnp
from jax import lax
from jax.experimental import pallas as pl
from jax.experimental.pallas import tpu as pltpu
from jax.sharding import PartitionSpec as P

STEP = 0.06
NT = 128
NS = 4
ROWS = 16
EXT = 24
COLS = 2048
MESH = pl.DeviceIdType.MESH
NCOPY = 112


def apply(v, weights, rows=EXT):
    vl = pltpu.roll(v[:rows], 1, axis=1)
    vr = pltpu.roll(v[:rows], COLS - 1, axis=1)
    above = pltpu.roll(v, 1, axis=0)[:rows]
    below = pltpu.roll(v, EXT - 1, axis=0)[:rows]

    def w(i):
        return weights[i, 0:rows]

    return w(0) * v[:rows] + w(1) * above + w(2) * below + (w(3) * vl + w(4) * vr)


class Batch:
    def __init__(self, core, copies, sender=None, receiver=None):
        self.core, self.copies, self.sender, self.receiver = core, copies, sender, receiver

    def each(self, only, act):
        if only is None:
            for c in self.copies:
                act(c)
        else:

            @pl.when(self.core == only)
            def _():
                for c in self.copies:
                    act(c)

    def start(self):
        self.each(self.sender, lambda c: c.start())

    def arrive(self):
        self.each(self.receiver, lambda c: c.wait_recv())

    def sent(self):
        self.each(self.sender, lambda c: c.wait_send())


def kernel(
    forcing, iterate, perm, out,
    f_buf, i_buf, k_buf, w_fine, w_mid, ahead, r_buf, b_buf, g_buf, pg, ppg, ge_in,
    u_buf, u_in, y_buf, yc, m1, m1_in, q_buf, m2, m2_in, x_buf, base, o_buf,
    send, recv, local, out_sem,
):
    t = lax.axis_index("tm")
    s = lax.axis_index("space")
    core = lax.rem(t, 2)
    chip = t // 2
    up = lax.rem(s + NS - 1, NS)
    down = lax.rem(s + 1, NS)
    mate = t + 1 - 2 * core
    count = [0]
    batches = []

    def shift(by):
        return lax.rem(t + by + NT, NT)

    def remote(src, dst, tm, sp):
        i = count[0]
        count[0] += 1
        return pltpu.make_async_remote_copy(
            src_ref=src, dst_ref=dst, send_sem=send.at[i], recv_sem=recv.at[i],
            device_id=(tm, sp), device_id_type=MESH,
        )

    def edges(src, dst, tm, depth):
        return [
            remote(src.at[0:depth], dst.at[ROWS : ROWS + depth], tm, up),
            remote(src.at[ROWS - depth : ROWS], dst.at[EXT - depth : EXT], tm, down),
        ]

    def batch(copies, sender=None, receiver=None):
        made = Batch(core, copies, sender, receiver)
        batches.append(made)
        made.start()
        return made

    loads = [pltpu.make_async_copy(perm, k_buf.at[0:ROWS], local.at[0])]
    for p in range(4):
        loads.append(pltpu.make_async_copy(iterate.at[p], i_buf.at[p, 0:ROWS], local.at[1 + p]))
        loads.append(
            pltpu.make_async_copy(
                forcing.at[4 * p : 4 * p + 4], f_buf.at[4 * p : 4 * p + 4, 0:ROWS], local.at[5 + p]
            )
        )
    for c in loads:
        c.start()

    barrier = pltpu.get_barrier_semaphore()

    def greet(tm, sp):
        pl.semaphore_signal(barrier, inc=1, device_id=(tm, sp), device_id_type=MESH)

    greet(t, up)
    greet(t, down)
    greet(mate, s)
    for by in (-2, -4):
        for sp in (s, up, down):
            greet(shift(by), sp)

    @pl.when(core == 0)
    def _():
        for sp in (s, up, down):
            greet(shift(-3), sp)

    @pl.when(core == 1)
    def _():
        greet(shift(-3), s)
        for sp in (up, down):
            greet(mate, sp)

    pl.semaphore_wait(barrier, 12)

    k_halo = batch(edges(perm, k_buf, t, 4))
    halo = []
    for p in range(4):
        one = edges(iterate.at[p], i_buf.at[p], t, 4)
        for j in (1, 2, 3):
            one += edges(forcing.at[4 * p + j], f_buf.at[4 * p + j], t, 4 - j)
        if p == 0:
            one += edges(forcing.at[0], f_buf.at[0], t, 3)
        halo.append(batch(one))

    for c in loads:
        c.wait()
    k_halo.arrive()

    row = lax.broadcasted_iota(jnp.int32, (EXT, 128), 0)
    is_below = jnp.logical_and(row >= ROWS, row < ROWS + 4)
    is_above = row >= ROWS + 4
    outside = jnp.logical_or(
        jnp.logical_and(is_below, s == NS - 1), jnp.logical_and(is_above, s == 0)
    )
    inside = jnp.where(outside, 0.0, 1.0).astype(jnp.float32)
    lane = lax.broadcasted_iota(jnp.int32, (EXT, 128), 1)
    in_above = pltpu.roll(inside, 1, axis=0) * inside
    in_below = pltpu.roll(inside, EXT - 1, axis=0) * inside
    for j in range(COLS // 128):
        at = slice(128 * j, 128 * j + 128)
        k = k_buf[:, at] * inside
        zero = jnp.zeros_like(k)
        kl = k_buf[:, 128 * j - 128 : 128 * j] * inside if j else zero
        kr = k_buf[:, 128 * j + 128 : 128 * j + 256] * inside if j < COLS // 128 - 1 else zero
        k_left = jnp.where(lane == 0, pltpu.roll(kl, 1, axis=1), pltpu.roll(k, 1, axis=1))
        k_right = jnp.where(lane == 127, pltpu.roll(kr, 127, axis=1), pltpu.roll(k, 127, axis=1))
        wa = 0.5 * (k + pltpu.roll(k, 1, axis=0))
        wb = 0.5 * (k + pltpu.roll(k, EXT - 1, axis=0))
        wl = 0.5 * (k + k_left)
        wr = 0.5 * (k + k_right)
        total = (wa + wb) + (wl + wr)
        if j == 0:
            wl = jnp.where(lane == 0, 0.0, wl)
        if j == COLS // 128 - 1:
            wr = jnp.where(lane == 127, 0.0, wr)
        for ref, c in ((w_fine, STEP), (w_mid, 4.0 * STEP)):
            ref[0, :, at] = 1.0 - c * total
            ref[1, :, at] = c * (wa * in_above)
            ref[2, :, at] = c * (wb * in_below)
            ref[3, :, at] = c * wl
            ref[4, :, at] = c * wr

    r_halo = []
    for p in range(4):
        halo[p].arrive()
        state = i_buf[p]
        for j in (1, 2, 3):
            state = apply(state, w_fine) + f_buf[4 * p + j]
        last = apply(state, w_fine, ROWS)
        if p < 3:
            r_buf[p, 0:ROWS] = f_buf[4 * p + 4, 0:ROWS] + last - i_buf[p + 1, 0:ROWS]
            r_halo.append(batch(edges(r_buf.at[p], r_buf.at[p], t, 3 - p)))
        else:
            ahead[...] = last
        if p == 0:
            g = f_buf[0] - i_buf[0]
            g_buf[...] = g
            early = batch([remote(g_buf, ge_in, shift(3), s)], 0, 1)
            pg[...] = apply(g, w_mid)

            @pl.when(core == 0)
            def _():
                ppg[...] = apply(pg[...], w_mid, ROWS)

            early_mate = batch([remote(ppg, ppg, mate, s)], 0, 1)

    r_halo[0].arrive()
    r_halo[1].arrive()
    b_buf[0] = apply(r_buf[0], w_mid) + r_buf[1]
    r_halo[2].arrive()
    b_buf[1] = apply(b_buf[0], w_mid) + r_buf[2]
    u = apply(b_buf[1], w_mid, ROWS) + ahead[...]
    u_buf[...] = u
    y_buf[core, 0:ROWS] = u + pg[0:ROWS]

    y_edges = batch(edges(y_buf.at[0], y_buf.at[0], t, 1), 0, 0)
    y_cross = batch(edges(y_buf.at[0], y_buf.at[0], mate, 1), 0, 1)
    y_main = batch([remote(y_buf.at[core, 0:ROWS], y_buf.at[core, 0:ROWS], mate, s)])
    u_far = batch(edges(u_buf, u_in, shift(3), 4) + [remote(u_buf, u_in.at[0:ROWS], shift(3), s)], 1, 0)

    base[0] = i_buf[1, 0:ROWS] + r_buf[0, 0:ROWS]
    base[1] = i_buf[2, 0:ROWS] + b_buf[0, 0:ROWS]
    base[2] = i_buf[3, 0:ROWS] + b_buf[1, 0:ROWS]

    early.arrive()
    early_mate.arrive()
    y_main.arrive()
    y_cross.arrive()
    y_edges.arrive()
    odd = core.astype(jnp.float32)
    both = apply(y_buf[0], w_mid, ROWS) + y_buf[1, 0:ROWS]
    yc[...] = both
    m1[...] = both - odd * ppg[...]
    m1_copies = batch(edges(m1, m1_in, shift(2), 2) + [remote(m1, m1_in.at[0:ROWS], shift(2), s)])

    one = jnp.where(chip >= 1, 1.0, 0.0).astype(jnp.float32)
    two = jnp.where(chip >= 2, 1.0, 0.0).astype(jnp.float32)

    u_far.arrive()

    @pl.when(core == 0)
    def _():
        q_buf[...] = two * apply(apply(u_in[...], w_mid), w_mid)

    @pl.when(core == 1)
    def _():
        q_buf[...] = jnp.zeros_like(q_buf)

    m1_copies.arrive()
    near = one * m1_in[...] + q_buf[...]
    m2[...] = apply(apply(near, w_mid), w_mid, ROWS) + yc[...]
    m2_copies = batch(edges(m2, m2_in, shift(4), 3) + [remote(m2, m2_in.at[0:ROWS], shift(4), s)])
    m2_copies.arrive()

    @pl.when(core == 0)
    def _():
        far = apply(apply(m2_in[...], w_mid), w_mid, ROWS)
        x_buf[0:ROWS] = g_buf[0:ROWS] + one * m1_in[0:ROWS] + two * far

    @pl.when(core == 1)
    def _():
        far = two * m2_in[...] + one * ge_in[...]
        far = apply(apply(far, w_mid), w_mid) + one * m1_in[...]
        x_buf[0:ROWS] = g_buf[0:ROWS] + y_buf[0, 0:ROWS] + apply(far, w_mid, ROWS)

    x_copies = batch(edges(x_buf, x_buf, t, 3))
    outs = [pltpu.make_async_copy(o_buf.at[j], out.at[j], out_sem.at[j]) for j in range(4)]
    o_buf[0] = i_buf[0, 0:ROWS] + x_buf[0:ROWS]
    outs[0].start()
    x_copies.arrive()

    state = x_buf[...]
    for j in (1, 2, 3):
        state = apply(state, w_mid, EXT if j < 3 else ROWS)
        o_buf[j] = base[j - 1] + state[:ROWS]
        outs[j].start()

    for c in outs:
        c.wait()
    for b in batches:
        b.sent()


def per_device(forcing, iterate, permeability):
    def field(*lead, rows=EXT):
        return pltpu.VMEM((*lead, rows, COLS), jnp.float32)

    scratch = [
        field(16),
        field(4),
        field(),
        field(5),
        field(5),
        field(rows=ROWS),
        field(3),
        field(2),
        field(),
        field(),
        field(rows=ROWS),
        field(),
        field(rows=ROWS),
        field(),
        field(2),
        field(rows=ROWS),
        field(rows=ROWS),
        field(),
        field(),
        field(rows=ROWS),
        field(),
        field(),
        field(3, rows=ROWS),
        field(4, rows=ROWS),
        pltpu.SemaphoreType.DMA((NCOPY,)),
        pltpu.SemaphoreType.DMA((NCOPY,)),
        pltpu.SemaphoreType.DMA((9,)),
        pltpu.SemaphoreType.DMA((4,)),
    ]
    return pl.pallas_call(
        kernel,
        name="vcycle",
        out_shape=jax.ShapeDtypeStruct(iterate.shape, iterate.dtype),
        in_specs=[pl.BlockSpec(memory_space=pl.ANY)] * 3,
        out_specs=pl.BlockSpec(memory_space=pl.ANY),
        scratch_shapes=scratch,
        compiler_params=pltpu.CompilerParams(
            collective_id=0, has_side_effects=True, vmem_limit_bytes=40 * 2**20
        ),
    )(forcing, iterate, permeability)


def solution(mesh):
    in_specs = (P("tm", "space", None), P("tm", "space", None), P("space", None))
    out_specs = P("tm", "space", None)
    return jax.shard_map(
        per_device, mesh=mesh, in_specs=in_specs, out_specs=out_specs, check_vma=False
    )
```

time: 64.9 us -> 59.5 us (0.917)
  Pallas kernels: 60.3 us -> 55 us
    pallas_call x1, Pallas kernels: 60.3 us -> 55 us  [per_device(): pl.pallas_call(kernel, name='vcycle', out_shape=jax.ShapeDtypeStruct(iter...]
where the time goes in v2:
time: 59.5 us; the launch traced here: 59.3 us
  Pallas kernels  55 us (92%)
  local copies, waits for them, and re-layouts  4.33 us (7%)
    pallas_call x1, Pallas kernels, per_device(): pl.pallas_call(kernel, name='vcycle', out_shape=jax.ShapeDtypeStruct(iter...  55 us
    unnamed x7, local copies, waits for them, and re-layouts  4.33 us

profile of v2, /device:TPU:1, one launch (start us, length us, event | category | flops | bytes accessed | tf_op | source)
XLA Modules:
  0.0 59.3 jit_solution(3730688331990695117)
XLA Ops:
  0.0 0.0 copy-start
  0.0 1.6 %copy-done = f32[16,16,2048]{2,1,0:T(8,128)S(1)} copy-done((f32[16,16,2048]{2,1,0:T(8,128)S(1)}, f32[16,16,2048]{2,1,0:T(8,128)}, u32[]{:S(2)}) %copy-start) | copy-done | bytes 2097176
  1.6 0.0 copy-start.1
  1.6 1.0 %copy-done.1 = f32[4,16,2048]{2,1,0:T(8,128)S(1)} copy-done((f32[4,16,2048]{2,1,0:T(8,128)S(1)}, f32[4,16,2048]{2,1,0:T(8,128)}, u32[]{:S(2)}) %copy-start.1) | copy-done | bytes 524312
  2.6 0.0 copy-start.2
  2.6 0.9 %copy-done.2 = f32[16,2048]{1,0:T(8,128)S(1)} copy-done((f32[16,2048]{1,0:T(8,128)S(1)}, f32[16,2048]{1,0:T(8,128)}, u32[]{:S(2)}) %copy-start.2) | copy-done | bytes 131096
  3.5 55.0 %vcycle.1 = f32[4,16,2048]{2,1,0:T(8,128)S(1)} custom-call(f32[16,16,2048]{2,1,0:T(8,128)S(1)} %copy-done, f32[4,16,2048]{2,1,0:T(8,128)S(1)} %copy-done.1, f32[16,2048]{1,0:T(8,128)S(1)} %copy-done.2), custom_call_target="tpu_custom_call" | custom-call | tf_op jit(solution)/shard_map/vcycle/pallas_call | solution.py:313
  58.5 0.8 %copy.5 = f32[4,16,2048]{2,1,0:T(8,128)} copy(f32[4,16,2048]{2,1,0:T(8,128)S(1)} %vcycle.1) | data formatting | bytes 1048576
Async XLA Ops:
  0.0 1.6 %copy-start = (f32[16,16,2048]{2,1,0:T(8,128)S(1)}, f32[16,16,2048]{2,1,0:T(8,128)}, u32[]{:S(2)}) copy-start(f32[16,16,2048]{2,1,0:T(8,128)} %forcing.1) | copy-start | bytes 6291460
  1.6 1.0 %copy-start.1 = (f32[4,16,2048]{2,1,0:T(8,128)S(1)}, f32[4,16,2048]{2,1,0:T(8,128)}, u32[]{:S(2)}) copy-start(f32[4,16,2048]{2,1,0:T(8,128)} %iterate.1) | copy-start | bytes 1572868
  2.6 0.9 %copy-start.2 = (f32[16,2048]{1,0:T(8,128)S(1)}, f32[16,2048]{1,0:T(8,128)}, u32[]{:S(2)}) copy-start(f32[16,2048]{1,0:T(8,128)} %perm.1) | copy-start | bytes 393220

commit v3 on v0

v3 whole, which is shorter than its diff:
```python
import jax
import jax.numpy as jnp
from jax import lax
from jax.experimental import pallas as pl
from jax.experimental.pallas import tpu as pltpu
from jax.sharding import PartitionSpec as P

STEP = 0.06
NT = 128
NS = 4
ROWS = 16
COLS = 2048
HALF = 1024
WIN = 1152
MESH = pl.DeviceIdType.MESH
NCOPY = 48


def apply(v, weights, at=None):
    rows, cols = v.shape
    vl = pltpu.roll(v, 1, axis=1)
    vr = pltpu.roll(v, cols - 1, axis=1)
    above = pltpu.roll(v, 1, axis=0)
    below = pltpu.roll(v, rows - 1, axis=0)

    def w(i):
        return weights[i] if at is None else weights[i, :, pl.ds(at, cols)]

    return w(0) * v + w(1) * above + w(2) * below + (w(3) * vl + w(4) * vr)


def extend(v, rows):
    return jnp.concatenate([v, jnp.zeros((rows - ROWS, v.shape[1]), v.dtype)], axis=0)


def widen(v):
    rim = v[ROWS : ROWS + 8]
    near = lax.broadcasted_iota(jnp.int32, rim.shape, 0) < 4
    zero = jnp.zeros_like(rim)
    return jnp.concatenate([v[0:ROWS], jnp.where(near, rim, zero), jnp.where(near, zero, rim)], axis=0)


def kernel(
    forcing, iterate, perm, out,
    f_buf, i_buf, k_buf, w_fine, w_mid, w_wide, r_buf, b_buf, g_buf, pg, u_buf, cu, cb, cpg, far_src, far_in,
    y_buf, yw, m1_in, m2, m2_in, z_buf, w_buf, x_buf, cx, xh, o_buf,
    send, recv, local, out_sem,
):
    t = lax.axis_index("tm")
    s = lax.axis_index("space")
    core = lax.rem(t, 2)
    chip = t // 2
    up = lax.rem(s + NS - 1, NS)
    down = lax.rem(s + 1, NS)
    mate = t + 1 - 2 * core
    count = [0]
    batches = []

    def shift(by):
        return lax.rem(t + by + NT, NT)

    def remote(src, dst, tm, sp):
        i = count[0]
        count[0] += 1
        return pltpu.make_async_remote_copy(
            src_ref=src, dst_ref=dst, send_sem=send.at[i], recv_sem=recv.at[i],
            device_id=(tm, sp), device_id_type=MESH,
        )

    def batch(copies):
        for c in copies:
            c.start()
        batches.append(copies)
        return copies

    def arrive(copies):
        for c in copies:
            c.wait_recv()

    loads = [
        pltpu.make_async_copy(perm, k_buf.at[0:ROWS], local.at[0]),
        pltpu.make_async_copy(iterate, i_buf, local.at[1]),
        pltpu.make_async_copy(forcing, f_buf, local.at[2]),
    ]
    for c in loads:
        c.start()

    barrier = pltpu.get_barrier_semaphore()
    for tm, sp in ((t, up), (t, down), (mate, s), (shift(-2), s), (shift(-4), s), (shift(-7), s)):
        pl.semaphore_signal(barrier, inc=1, device_id=(tm, sp), device_id_type=MESH)

    m1_in[ROWS + 1 : 23] = jnp.zeros((6, WIN), jnp.float32)
    m2_in[ROWS + 3 : 21] = jnp.zeros((2, WIN), jnp.float32)
    xh[3:5] = jnp.zeros((2, COLS), jnp.float32)
    pl.semaphore_wait(barrier, 6)

    k_halo = batch([
        remote(perm.at[0:8], k_buf.at[16:24], t, up),
        remote(perm.at[8:16], k_buf.at[24:32], t, down),
    ])
    for c in loads:
        c.wait()
    g_buf[...] = f_buf[0] - i_buf[0]
    far = [remote(far_src, far_in, shift(7), s)]
    batches.append(far)

    @pl.when(core == 0)
    def _():
        far_src[...] = g_buf[...]
        far[0].start()

    arrive(k_halo)

    row = lax.broadcasted_iota(jnp.int32, (32, 128), 0)
    is_below = jnp.logical_and(row >= ROWS, row < ROWS + 8)
    is_above = row >= ROWS + 8
    outside = jnp.logical_or(
        jnp.logical_and(is_below, s == NS - 1), jnp.logical_and(is_above, s == 0)
    )
    inside = jnp.where(outside, 0.0, 1.0).astype(jnp.float32)
    lane = lax.broadcasted_iota(jnp.int32, (32, 128), 1)
    in_above = pltpu.roll(inside, 1, axis=0) * inside
    in_below = pltpu.roll(inside, 31, axis=0) * inside
    near = lax.broadcasted_iota(jnp.int32, (8, 128), 0) < 4

    def narrow(v):
        return jnp.concatenate([v[0:ROWS], jnp.where(near, v[16:24], v[24:32])], axis=0)

    for j in range(COLS // 128):
        at = slice(128 * j, 128 * j + 128)
        k = k_buf[:, at] * inside
        zero = jnp.zeros_like(k)
        kl = k_buf[:, 128 * j - 128 : 128 * j] * inside if j else zero
        kr = k_buf[:, 128 * j + 128 : 128 * j + 256] * inside if j < COLS // 128 - 1 else zero
        k_left = jnp.where(lane == 0, pltpu.roll(kl, 1, axis=1), pltpu.roll(k, 1, axis=1))
        k_right = jnp.where(lane == 127, pltpu.roll(kr, 127, axis=1), pltpu.roll(k, 127, axis=1))
        wa = 0.5 * (k + pltpu.roll(k, 1, axis=0))
        wb = 0.5 * (k + pltpu.roll(k, 31, axis=0))
        wl = 0.5 * (k + k_left)
        wr = 0.5 * (k + k_right)
        total = (wa + wb) + (wl + wr)
        wa = wa * in_above
        wb = wb * in_below
        if j == 0:
            wl = jnp.where(lane == 0, 0.0, wl)
        if j == COLS // 128 - 1:
            wr = jnp.where(lane == 127, 0.0, wr)
        for i, v in enumerate((total, wa, wb, wl, wr)):
            fine = 1.0 - STEP * v if i == 0 else STEP * v
            mid = 1.0 - 4.0 * STEP * v if i == 0 else 4.0 * STEP * v
            w_fine[i, :, at] = narrow(fine)
            w_mid[i, :, at] = narrow(mid)
            w_wide[i, :, at] = mid

    pg[...] = apply(extend(g_buf[...], 24), w_mid)
    pg_halo = batch([
        remote(pg.at[16:17], cpg.at[0], t, down),
        remote(pg.at[23:24], cpg.at[1], t, up),
    ])

    for p in range(4):
        state = extend(i_buf[p], 24)
        for j in (1, 2, 3):
            state = apply(state, w_fine) + extend(f_buf[4 * p + j], 24)
        state = apply(state, w_fine)
        if p < 3:
            r_buf[p] = state + extend(f_buf[4 * p + 4] - i_buf[p + 1], 24)
        else:
            r_buf[3] = state

    b_buf[0] = widen(r_buf[0])
    b_buf[1] = apply(b_buf[0], w_wide) + widen(r_buf[1])
    b_buf[2] = apply(b_buf[1], w_wide) + widen(r_buf[2])
    u_buf[...] = apply(b_buf[2], w_wide) + widen(r_buf[3])
    u_rim = batch([
        remote(u_buf.at[16:24], cu.at[0:8], t, down),
        remote(u_buf.at[24:32], cu.at[8:16], t, up),
    ])
    b_rim = []
    for j in range(3):
        b_rim += batch([
            remote(b_buf.at[j, 16:24], cb.at[j, 0:8], t, down),
            remote(b_buf.at[j, 24:32], cb.at[j, 8:16], t, up),
        ])
    arrive(pg_halo)
    pg[0:1] = pg[0:1] + cpg[0]
    pg[15:16] = pg[15:16] + cpg[1]
    arrive(u_rim)
    u = u_buf[0:ROWS] + cu[...]
    y_buf[core] = u + pg[0:ROWS]

    y_swap = batch([remote(y_buf.at[core], y_buf.at[core], mate, s)])

    @pl.when(core == 1)
    def _():
        far_src[...] = u

    arrive(y_swap)

    start = pl.multiple_of(core * (COLS - WIN), 128)
    window = pl.ds(start, WIN)
    yw[...] = apply(extend(y_buf[0, :, window], 24), w_mid, start) + extend(y_buf[1, :, window], 24)
    m1_copies = batch([
        remote(yw.at[0:ROWS], m1_in.at[0:ROWS], shift(2), s),
        remote(yw.at[16:17], m1_in.at[16:17], shift(2), s),
        remote(yw.at[23:24], m1_in.at[23:24], shift(2), s),
    ])

    @pl.when(core == 1)
    def _():
        far[0].start()

    one = jnp.where(chip >= 1, 1.0, 0.0).astype(jnp.float32)
    two = jnp.where(chip >= 2, 1.0, 0.0).astype(jnp.float32)
    arrive(m1_copies)
    m2[...] = one * apply(apply(m1_in[...], w_mid, start), w_mid, start) + yw[...]
    m2_copies = batch([
        remote(m2.at[0:ROWS], m2_in.at[0:ROWS], shift(4), s),
        remote(m2.at[16:19], m2_in.at[16:19], shift(4), s),
        remote(m2.at[21:24], m2_in.at[21:24], shift(4), s),
    ])

    arrive(b_rim)
    for j in range(3):
        o_buf[j + 1] = i_buf[j + 1] + (b_buf[j, 0:ROWS] + cb[j])
    arrive(far)
    use6 = jnp.where(jnp.logical_and(core == 0, chip >= 4), 1.0, 0.0).astype(jnp.float32)
    use7 = jnp.where(jnp.logical_and(core == 1, chip >= 3), -1.0, 0.0).astype(jnp.float32)
    odd = core.astype(jnp.float32)
    z = extend(far_in[...], 32)
    for _ in range(6):
        z = apply(z, w_wide)
    z_buf[...] = use6 * z + use7 * apply(z, w_wide) + extend(g_buf[...] + odd * y_buf[0], 32)
    arrive(m2_copies)
    wide = apply(apply(widen(m2_in[...]), w_wide, start), w_wide, start)
    wide = one * widen(m1_in[...]) + two * wide
    left = wide[:, 0:HALF]
    right = wide[:, WIN - HALF : WIN]

    @pl.when(core == 0)
    def _():
        w_buf[:, 0:HALF] = left

    @pl.when(core == 1)
    def _():
        w_buf[:, HALF:COLS] = right

    half = pl.ds(pl.multiple_of(core * HALF, 128), HALF)
    w_swap = batch([remote(w_buf.at[:, half], w_buf.at[:, half], mate, s)])
    arrive(w_swap)

    @pl.when(core == 0)
    def _():
        x_buf[...] = z_buf[...] + w_buf[...]

    @pl.when(core == 1)
    def _():
        x_buf[...] = z_buf[...] + apply(w_buf[...], w_wide)

    x_rim = batch([
        remote(x_buf.at[16:24], cx.at[0:8], t, down),
        remote(x_buf.at[24:32], cx.at[8:16], t, up),
        remote(x_buf.at[0:3], xh.at[0:3], t, up),
        remote(x_buf.at[13:16], xh.at[5:8], t, down),
    ])
    outs = [pltpu.make_async_copy(o_buf.at[j], out.at[j], out_sem.at[j]) for j in range(4)]
    arrive(x_rim)
    x = x_buf[0:ROWS] + cx[...]
    rim = lax.broadcasted_iota(jnp.int32, (8, COLS), 0) < 4
    state = jnp.concatenate([x, jnp.where(rim, x_buf[16:24], x_buf[24:32]) + xh[...]], axis=0)
    o_buf[0] = i_buf[0] + x
    outs[0].start()

    for j in (1, 2, 3):
        state = apply(state, w_mid)
        o_buf[j] = o_buf[j] + state[0:ROWS]
        outs[j].start()
    for c in outs:
        c.wait()
    for copies in batches:
        for c in copies:
            c.wait_send()


def per_device(forcing, iterate, permeability):
    def field(*shape):
        return pltpu.VMEM(shape, jnp.float32)

    scratch = [
        field(16, ROWS, COLS),
        field(4, ROWS, COLS),
        field(32, COLS),
        field(5, 24, COLS),
        field(5, 24, COLS),
        field(5, 32, COLS),
        field(4, 24, COLS),
        field(3, 32, COLS),
        field(ROWS, COLS),
        field(24, COLS),
        field(32, COLS),
        field(ROWS, COLS),
        field(3, ROWS, COLS),
        field(2, 1, COLS),
        field(ROWS, COLS),
        field(ROWS, COLS),
        field(2, ROWS, COLS),
        field(24, WIN),
        field(24, WIN),
        field(24, WIN),
        field(24, WIN),
        field(32, COLS),
        field(32, COLS),
        field(32, COLS),
        field(ROWS, COLS),
        field(8, COLS),
        field(4, ROWS, COLS),
        pltpu.SemaphoreType.DMA((NCOPY,)),
        pltpu.SemaphoreType.DMA((NCOPY,)),
        pltpu.SemaphoreType.DMA((3,)),
        pltpu.SemaphoreType.DMA((4,)),
    ]
    return pl.pallas_call(
        kernel,
        name="vcycle",
        out_shape=jax.ShapeDtypeStruct(iterate.shape, iterate.dtype),
        in_specs=[pl.BlockSpec(memory_space=pl.ANY)] * 3,
        out_specs=pl.BlockSpec(memory_space=pl.ANY),
        scratch_shapes=scratch,
        compiler_params=pltpu.CompilerParams(
            collective_id=0, has_side_effects=True, vmem_limit_bytes=60 * 2**20
        ),
    )(forcing, iterate, permeability)


def solution(mesh):
    in_specs = (P("tm", "space", None), P("tm", "space", None), P("space", None))
    out_specs = P("tm", "space", None)
    return jax.shard_map(
        per_device, mesh=mesh, in_specs=in_specs, out_specs=out_specs, check_vma=False
    )
```

time: 211 us -> 49.4 us (0.23)
  the two profiles are of different devices: /device:TPU:6 before, /device:TPU:1 now
where the time goes in v3:
time: 49.4 us; the launch traced here: 49.2 us
  Pallas kernels  47.3 us (96%)
  local copies, waits for them, and re-layouts  1.87 us (4%)
    pallas_call x1, Pallas kernels, per_device(): pl.pallas_call(kernel, name='vcycle', out_shape=jax.ShapeDtypeStruct(iter...  47.3 us
    unnamed x1, local copies, waits for them, and re-layouts  1.87 us

profile of v3, /device:TPU:1, one launch (start us, length us, event | category | flops | bytes accessed | tf_op | source)
XLA Modules:
  0.0 49.2 jit_solution(3483469368374702796)
XLA Ops:
  0.0 47.3 %vcycle.1 = f32[4,16,2048]{2,1,0:T(8,128)} custom-call(f32[16,16,2048]{2,1,0:T(8,128)} %forcing.1, f32[4,16,2048]{2,1,0:T(8,128)} %iterate.1, f32[16,2048]{1,0:T(8,128)} %perm.1), custom_call_target="tpu_custom_call" | custom-call | tf_op jit(solution)/shard_map/vcycle/pallas_call | solution.py:322
  47.3 1.9 %copy.5 = f32[4,16,2048]{2,1,0:T(8,128)} copy(f32[4,16,2048]{2,1,0:T(8,128)} %vcycle.1) | data formatting | bytes 1048576

commit v4 on v3

--- a/solution.py
+++ b/solution.py
@@ -42,9 +42,9 @@
 
 def kernel(
     forcing, iterate, perm, out,
-    f_buf, i_buf, k_buf, w_fine, w_mid, w_wide, r_buf, b_buf, g_buf, pg, u_buf, cu, cb, cpg, far_src, far_in,
-    y_buf, yw, m1_in, m2, m2_in, z_buf, w_buf, x_buf, cx, xh, o_buf,
-    send, recv, local, out_sem,
+    f_buf, i_buf, k_buf, w_fine, w_mid, w_wide, s_buf, r_buf, b_buf, g_buf, pg, u_buf, cu, cb, cpg, far_src, far_in,
+    y_buf, yw, m1_in, m2, m2_in, z_buf, cz, hz, za, w_buf, cw, hw, w_sum, base,
+    send, recv, local,
 ):
     t = lax.axis_index("tm")
     s = lax.axis_index("space")
@@ -86,13 +86,16 @@
         c.start()
 
     barrier = pltpu.get_barrier_semaphore()
-    for tm, sp in ((t, up), (t, down), (mate, s), (shift(-2), s), (shift(-4), s), (shift(-7), s)):
+    for tm, sp in (
+        (t, up), (t, down), (mate, s), (mate, up), (mate, down), (shift(-2), s), (shift(-4), s), (shift(-7), s)
+    ):
         pl.semaphore_signal(barrier, inc=1, device_id=(tm, sp), device_id_type=MESH)
 
     m1_in[ROWS + 1 : 23] = jnp.zeros((6, WIN), jnp.float32)
     m2_in[ROWS + 3 : 21] = jnp.zeros((2, WIN), jnp.float32)
-    xh[3:5] = jnp.zeros((2, COLS), jnp.float32)
-    pl.semaphore_wait(barrier, 6)
+    hz[3:5] = jnp.zeros((2, COLS), jnp.float32)
+    cw[:, 5:11] = jnp.zeros((2, 6, HALF), jnp.float32)
+    pl.semaphore_wait(barrier, 8)
 
     k_halo = batch([
         remote(perm.at[0:8], k_buf.at[16:24], t, up),
@@ -158,15 +161,15 @@
         remote(pg.at[23:24], cpg.at[1], t, up),
     ])
 
-    for p in range(4):
-        state = extend(i_buf[p], 24)
-        for j in (1, 2, 3):
-            state = apply(state, w_fine) + extend(f_buf[4 * p + j], 24)
-        state = apply(state, w_fine)
-        if p < 3:
-            r_buf[p] = state + extend(f_buf[4 * p + 4] - i_buf[p + 1], 24)
-        else:
-            r_buf[3] = state
+    for j in (1, 2, 3, 4):
+        for p in range(4):
+            state = apply(extend(i_buf[p], 24) if j == 1 else s_buf[j % 2, p], w_fine)
+            if j < 4:
+                s_buf[1 - j % 2, p] = state + extend(f_buf[4 * p + j], 24)
+            elif p < 3:
+                r_buf[p] = state + extend(f_buf[4 * p + 4] - i_buf[p + 1], 24)
+            else:
+                r_buf[3] = state
 
     b_buf[0] = widen(r_buf[0])
     b_buf[1] = apply(b_buf[0], w_wide) + widen(r_buf[1])
@@ -194,6 +197,7 @@
     @pl.when(core == 1)
     def _():
         far_src[...] = u
+        far[0].start()
 
     arrive(y_swap)
 
@@ -205,10 +209,6 @@
         remote(yw.at[16:17], m1_in.at[16:17], shift(2), s),
         remote(yw.at[23:24], m1_in.at[23:24], shift(2), s),
     ])
-
-    @pl.when(core == 1)
-    def _():
-        far[0].start()
 
     one = jnp.where(chip >= 1, 1.0, 0.0).astype(jnp.float32)
     two = jnp.where(chip >= 2, 1.0, 0.0).astype(jnp.float32)
@@ -222,7 +222,7 @@
 
     arrive(b_rim)
     for j in range(3):
-        o_buf[j + 1] = i_buf[j + 1] + (b_buf[j, 0:ROWS] + cb[j])
+        base[j] = i_buf[j + 1] + (b_buf[j, 0:ROWS] + cb[j])
     arrive(far)
     use6 = jnp.where(jnp.logical_and(core == 0, chip >= 4), 1.0, 0.0).astype(jnp.float32)
     use7 = jnp.where(jnp.logical_and(core == 1, chip >= 3), -1.0, 0.0).astype(jnp.float32)
@@ -231,52 +231,65 @@
     for _ in range(6):
         z = apply(z, w_wide)
     z_buf[...] = use6 * z + use7 * apply(z, w_wide) + extend(g_buf[...] + odd * y_buf[0], 32)
+    z_rim = batch([
+        remote(z_buf.at[16:24], cz.at[0:8], t, down),
+        remote(z_buf.at[24:32], cz.at[8:16], t, up),
+        remote(z_buf.at[0:3], hz.at[0:3], t, up),
+        remote(z_buf.at[13:16], hz.at[5:8], t, down),
+    ])
     arrive(m2_copies)
     wide = apply(apply(widen(m2_in[...]), w_wide, start), w_wide, start)
     wide = one * widen(m1_in[...]) + two * wide
-    left = wide[:, 0:HALF]
-    right = wide[:, WIN - HALF : WIN]
 
     @pl.when(core == 0)
     def _():
-        w_buf[:, 0:HALF] = left
+        w_buf[0] = wide[:, 0:HALF]
 
     @pl.when(core == 1)
     def _():
-        w_buf[:, HALF:COLS] = right
-
-    half = pl.ds(pl.multiple_of(core * HALF, 128), HALF)
-    w_swap = batch([remote(w_buf.at[:, half], w_buf.at[:, half], mate, s)])
+        w_buf[1] = wide[:, WIN - HALF : WIN]
+
+    mine = w_buf.at[core]
+    w_rim = []
+    for tm in (t, mate):
+        w_rim += [
+            remote(mine.at[16:21], cw.at[core, 0:5], tm, down),
+            remote(mine.at[27:32], cw.at[core, 11:16], tm, up),
+            remote(mine.at[0:4], hw.at[core, 0:4], tm, up),
+            remote(mine.at[12:16], hw.at[core, 4:8], tm, down),
+        ]
+    w_rim = batch(w_rim)
+    w_swap = batch([remote(mine, mine, mate, s)])
+
+    near = lax.broadcasted_iota(jnp.int32, (8, COLS), 0) < 4
+
+    def assemble(own, given, rim):
+        return jnp.concatenate(
+            [own[0:ROWS] + given, jnp.where(near, own[16:24], own[24:32]) + rim], axis=0
+        )
+
+    def halves(ref):
+        return jnp.concatenate([ref[0], ref[1]], axis=1)
+
+    arrive(z_rim)
+    za[...] = assemble(z_buf[...], cz[...], hz[...])
     arrive(w_swap)
+    arrive(w_rim)
+    w = assemble(halves(w_buf), halves(cw), halves(hw))
 
     @pl.when(core == 0)
     def _():
-        x_buf[...] = z_buf[...] + w_buf[...]
+        w_sum[...] = za[...] + w
 
     @pl.when(core == 1)
     def _():
-        x_buf[...] = z_buf[...] + apply(w_buf[...], w_wide)
-
-    x_rim = batch([
-        remote(x_buf.at[16:24], cx.at[0:8], t, down),
-        remote(x_buf.at[24:32], cx.at[8:16], t, up),
-        remote(x_buf.at[0:3], xh.at[0:3], t, up),
-        remote(x_buf.at[13:16], xh.at[5:8], t, down),
-    ])
-    outs = [pltpu.make_async_copy(o_buf.at[j], out.at[j], out_sem.at[j]) for j in range(4)]
-    arrive(x_rim)
-    x = x_buf[0:ROWS] + cx[...]
-    rim = lax.broadcasted_iota(jnp.int32, (8, COLS), 0) < 4
-    state = jnp.concatenate([x, jnp.where(rim, x_buf[16:24], x_buf[24:32]) + xh[...]], axis=0)
-    o_buf[0] = i_buf[0] + x
-    outs[0].start()
-
+        w_sum[...] = za[...] + apply(w, w_mid)
+
+    state = w_sum[...]
+    out[0] = i_buf[0] + state[0:ROWS]
     for j in (1, 2, 3):
         state = apply(state, w_mid)
-        o_buf[j] = o_buf[j] + state[0:ROWS]
-        outs[j].start()
-    for c in outs:
-        c.wait()
+        out[j] = base[j - 1] + state[0:ROWS]
     for copies in batches:
         for c in copies:
             c.wait_send()
@@ -293,6 +306,7 @@
         field(5, 24, COLS),
         field(5, 24, COLS),
         field(5, 32, COLS),
+        field(2, 4, 24, COLS),
         field(4, 24, COLS),
         field(3, 32, COLS),
         field(ROWS, COLS),
@@ -309,25 +323,27 @@
         field(24, WIN),
         field(24, WIN),
         field(32, COLS),
-        field(32, COLS),
-        field(32, COLS),
         field(ROWS, COLS),
         field(8, COLS),
-        field(4, ROWS, COLS),
+        field(24, COLS),
+        field(2, 32, HALF),
+        field(2, ROWS, HALF),
+        field(2, 8, HALF),
+        field(24, COLS),
+        field(3, ROWS, COLS),
         pltpu.SemaphoreType.DMA((NCOPY,)),
         pltpu.SemaphoreType.DMA((NCOPY,)),
         pltpu.SemaphoreType.DMA((3,)),
-        pltpu.SemaphoreType.DMA((4,)),
     ]
     return pl.pallas_call(
         kernel,
         name="vcycle",
         out_shape=jax.ShapeDtypeStruct(iterate.shape, iterate.dtype),
-        in_specs=[pl.BlockSpec(memory_space=pl.ANY)] * 3,
-        out_specs=pl.BlockSpec(memory_space=pl.ANY),
+        in_specs=[pl.BlockSpec(memory_space=pltpu.HBM)] * 3,
+        out_specs=pl.BlockSpec(memory_space=pltpu.VMEM),
         scratch_shapes=scratch,
         compiler_params=pltpu.CompilerParams(
-            collective_id=0, has_side_effects=True, vmem_limit_bytes=60 * 2**20
+            collective_id=0, has_side_effects=True, vmem_limit_bytes=int(53.25 * 2**20)
         ),
     )(forcing, iterate, permeability)
 

time: 49.4 us -> 47.7 us (0.966)
  Pallas kernels: 47.3 us -> 45.8 us
    pallas_call x1, Pallas kernels: 47.3 us -> 45.8 us  [per_device(): pl.pallas_call(kernel, name='vcycle', out_shape=jax.ShapeDtypeStruct(iter...]
    unnamed x1 -> x3, local copies, waits for them, and re-layouts: 1.87 us -> 1.7 us
where the time goes in v4:
time: 47.7 us; the launch traced here: 47.5 us
  Pallas kernels  45.8 us (96%)
  local copies, waits for them, and re-layouts  1.7 us (4%)
    pallas_call x1, Pallas kernels, per_device(): pl.pallas_call(kernel, name='vcycle', out_shape=jax.ShapeDtypeStruct(iter...  45.8 us
    unnamed x3, local copies, waits for them, and re-layouts  1.7 us

profile of v4, /device:TPU:1, one launch (start us, length us, event | category | flops | bytes accessed | tf_op | source)
XLA Modules:
  0.0 47.5 jit_solution(15296263495938342220)
XLA Ops:
  0.0 0.0 copy-start
  0.0 0.9 %copy-done = f32[16,2048]{1,0:T(8,128)S(1)} copy-done((f32[16,2048]{1,0:T(8,128)S(1)}, f32[16,2048]{1,0:T(8,128)}, u32[]{:S(2)}) %copy-start) | copy-done | bytes 131096
  0.9 45.8 %vcycle.1 = f32[4,16,2048]{2,1,0:T(8,128)S(1)} custom-call(f32[16,16,2048]{2,1,0:T(8,128)} %forcing.1, f32[4,16,2048]{2,1,0:T(8,128)} %iterate.1, f32[16,2048]{1,0:T(8,128)S(1)} %copy-done), custom_call_target="tpu_custom_call" | custom-call | tf_op jit(solution)/shard_map/vcycle/pallas_call | solution.py:338
  46.7 0.8 %copy.5 = f32[4,16,2048]{2,1,0:T(8,128)} copy(f32[4,16,2048]{2,1,0:T(8,128)S(1)} %vcycle.1) | data formatting | bytes 1048576
Async XLA Ops:
  0.0 0.9 %copy-start = (f32[16,2048]{1,0:T(8,128)S(1)}, f32[16,2048]{1,0:T(8,128)}, u32[]{:S(2)}) copy-start(f32[16,2048]{1,0:T(8,128)} %perm.1) | copy-start | bytes 393220

commit v5 on v4

--- a/solution.py
+++ b/solution.py
@@ -67,15 +67,36 @@
             device_id=(tm, sp), device_id_type=MESH,
         )
 
-    def batch(copies):
-        for c in copies:
-            c.start()
-        batches.append(copies)
+    def batch(copies, given=None):
+        batches.append((copies, given))
+        when(given, lambda: [c.start() for c in copies])
         return copies
 
-    def arrive(copies):
-        for c in copies:
-            c.wait_recv()
+    def when(given, act):
+        if given is None:
+            act()
+        else:
+            pl.when(given)(lambda: (act(), None)[1])
+
+    def arrive(copies, given=None):
+        when(given, lambda: [c.wait_recv() for c in copies])
+
+    chips = NT // 2
+    has1, has2 = chip >= 1, chip >= 2
+    has_far = chip >= 4 - core
+    to1, to2 = chip < chips - 1, chip < chips - 2
+    to_far = chip < chips - 3 - core
+
+    barrier = pltpu.get_barrier_semaphore()
+
+    def greet(tm, sp):
+        pl.semaphore_signal(barrier, inc=1, device_id=(tm, sp), device_id_type=MESH)
+
+    when(has_far, lambda: greet(shift(-7), s))
+    when(has2, lambda: greet(shift(-4), s))
+    when(has1, lambda: greet(shift(-2), s))
+    for tm, sp in ((mate, up), (mate, down), (t, up), (t, down), (mate, s)):
+        greet(tm, sp)
 
     loads = [
         pltpu.make_async_copy(perm, k_buf.at[0:ROWS], local.at[0]),
@@ -85,17 +106,26 @@
     for c in loads:
         c.start()
 
-    barrier = pltpu.get_barrier_semaphore()
-    for tm, sp in (
-        (t, up), (t, down), (mate, s), (mate, up), (mate, down), (shift(-2), s), (shift(-4), s), (shift(-7), s)
-    ):
-        pl.semaphore_signal(barrier, inc=1, device_id=(tm, sp), device_id_type=MESH)
-
     m1_in[ROWS + 1 : 23] = jnp.zeros((6, WIN), jnp.float32)
     m2_in[ROWS + 3 : 21] = jnp.zeros((2, WIN), jnp.float32)
     hz[3:5] = jnp.zeros((2, COLS), jnp.float32)
     cw[:, 5:11] = jnp.zeros((2, 6, HALF), jnp.float32)
-    pl.semaphore_wait(barrier, 8)
+
+    @pl.when(jnp.logical_not(has1))
+    def _():
+        m1_in[...] = jnp.zeros_like(m1_in)
+
+    @pl.when(jnp.logical_not(has2))
+    def _():
+        m2_in[...] = jnp.zeros_like(m2_in)
+
+    @pl.when(jnp.logical_not(has_far))
+    def _():
+        far_in[...] = jnp.zeros_like(far_in)
+
+    pl.semaphore_wait(
+        barrier, 5 + to1.astype(jnp.int32) + to2.astype(jnp.int32) + to_far.astype(jnp.int32)
+    )
 
     k_halo = batch([
         remote(perm.at[0:8], k_buf.at[16:24], t, up),
@@ -105,9 +135,9 @@
         c.wait()
     g_buf[...] = f_buf[0] - i_buf[0]
     far = [remote(far_src, far_in, shift(7), s)]
-    batches.append(far)
-
-    @pl.when(core == 0)
+    batches.append((far, to_far))
+
+    @pl.when(jnp.logical_and(core == 0, to_far))
     def _():
         far_src[...] = g_buf[...]
         far[0].start()
@@ -194,7 +224,7 @@
 
     y_swap = batch([remote(y_buf.at[core], y_buf.at[core], mate, s)])
 
-    @pl.when(core == 1)
+    @pl.when(jnp.logical_and(core == 1, to_far))
     def _():
         far_src[...] = u
         far[0].start()
@@ -208,38 +238,55 @@
         remote(yw.at[0:ROWS], m1_in.at[0:ROWS], shift(2), s),
         remote(yw.at[16:17], m1_in.at[16:17], shift(2), s),
         remote(yw.at[23:24], m1_in.at[23:24], shift(2), s),
-    ])
-
-    one = jnp.where(chip >= 1, 1.0, 0.0).astype(jnp.float32)
-    two = jnp.where(chip >= 2, 1.0, 0.0).astype(jnp.float32)
-    arrive(m1_copies)
-    m2[...] = one * apply(apply(m1_in[...], w_mid, start), w_mid, start) + yw[...]
+    ], to1)
+
+    z_rim = [
+        remote(z_buf.at[16:24], cz.at[0:8], t, down),
+        remote(z_buf.at[24:32], cz.at[8:16], t, up),
+        remote(z_buf.at[0:3], hz.at[0:3], t, up),
+        remote(z_buf.at[13:16], hz.at[5:8], t, down),
+    ]
+    batches.append((z_rim, None))
+
+    def far_term(more):
+        v = extend(far_in[...], 24)
+        for _ in range(4):
+            v = apply(v, w_mid)
+        v = widen(v)
+        for _ in range(more):
+            v = apply(v, w_wide)
+        return v
+
+    @pl.when(core == 1)
+    def _():
+        arrive(far, has_far)
+        z_buf[...] = extend(g_buf[...] + y_buf[0], 32) - far_term(3)
+        for c in z_rim:
+            c.start()
+
+
+    arrive(m1_copies, has1)
+    m2[...] = apply(apply(m1_in[...], w_mid, start), w_mid, start) + yw[...]
     m2_copies = batch([
         remote(m2.at[0:ROWS], m2_in.at[0:ROWS], shift(4), s),
         remote(m2.at[16:19], m2_in.at[16:19], shift(4), s),
         remote(m2.at[21:24], m2_in.at[21:24], shift(4), s),
-    ])
+    ], to2)
 
     arrive(b_rim)
     for j in range(3):
         base[j] = i_buf[j + 1] + (b_buf[j, 0:ROWS] + cb[j])
-    arrive(far)
-    use6 = jnp.where(jnp.logical_and(core == 0, chip >= 4), 1.0, 0.0).astype(jnp.float32)
-    use7 = jnp.where(jnp.logical_and(core == 1, chip >= 3), -1.0, 0.0).astype(jnp.float32)
-    odd = core.astype(jnp.float32)
-    z = extend(far_in[...], 32)
-    for _ in range(6):
-        z = apply(z, w_wide)
-    z_buf[...] = use6 * z + use7 * apply(z, w_wide) + extend(g_buf[...] + odd * y_buf[0], 32)
-    z_rim = batch([
-        remote(z_buf.at[16:24], cz.at[0:8], t, down),
-        remote(z_buf.at[24:32], cz.at[8:16], t, up),
-        remote(z_buf.at[0:3], hz.at[0:3], t, up),
-        remote(z_buf.at[13:16], hz.at[5:8], t, down),
-    ])
-    arrive(m2_copies)
+
+    @pl.when(core == 0)
+    def _():
+        arrive(far, has_far)
+        z_buf[...] = extend(g_buf[...], 32) + far_term(2)
+        for c in z_rim:
+            c.start()
+
+    arrive(m2_copies, has2)
     wide = apply(apply(widen(m2_in[...]), w_wide, start), w_wide, start)
-    wide = one * widen(m1_in[...]) + two * wide
+    wide = widen(m1_in[...]) + wide
 
     @pl.when(core == 0)
     def _():
@@ -290,9 +337,8 @@
     for j in (1, 2, 3):
         state = apply(state, w_mid)
         out[j] = base[j - 1] + state[0:ROWS]
-    for copies in batches:
-        for c in copies:
-            c.wait_send()
+    for copies, given in batches:
+        when(given, lambda: [c.wait_send() for c in copies])
 
 
 def per_device(forcing, iterate, permeability):

time: 47.7 us -> 44.7 us (0.937)
  the two profiles are of different devices: /device:TPU:1 before, /device:TPU:7 now
where the time goes in v5:
time: 44.7 us; the launch traced here: 44.6 us
  Pallas kernels  42.9 us (96%)
  local copies, waits for them, and re-layouts  1.7 us (4%)
    pallas_call x1, Pallas kernels, per_device(): pl.pallas_call(kernel, name='vcycle', out_shape=jax.ShapeDtypeStruct(iter...  42.9 us
    unnamed x3, local copies, waits for them, and re-layouts  1.7 us

profile of v5, /device:TPU:7, one launch (start us, length us, event | category | flops | bytes accessed | tf_op | source)
XLA Modules:
  0.0 44.6 jit_solution(2634180474792120610)
XLA Ops:
  0.0 0.0 copy-start
  0.0 0.9 %copy-done = f32[16,2048]{1,0:T(8,128)S(1)} copy-done((f32[16,2048]{1,0:T(8,128)S(1)}, f32[16,2048]{1,0:T(8,128)}, u32[]{:S(2)}) %copy-start) | copy-done | bytes 131096
  0.9 42.9 %vcycle.1 = f32[4,16,2048]{2,1,0:T(8,128)S(1)} custom-call(f32[16,16,2048]{2,1,0:T(8,128)} %forcing.1, f32[4,16,2048]{2,1,0:T(8,128)} %iterate.1, f32[16,2048]{1,0:T(8,128)S(1)} %copy-done), custom_call_target="tpu_custom_call" | custom-call | tf_op jit(solution)/shard_map/vcycle/pallas_call | solution.py:384
  43.8 0.8 %copy.5 = f32[4,16,2048]{2,1,0:T(8,128)} copy(f32[4,16,2048]{2,1,0:T(8,128)S(1)} %vcycle.1) | data formatting | bytes 1048576
Async XLA Ops:
  0.0 0.9 %copy-start = (f32[16,2048]{1,0:T(8,128)S(1)}, f32[16,2048]{1,0:T(8,128)}, u32[]{:S(2)}) copy-start(f32[16,2048]{1,0:T(8,128)} %perm.1) | copy-start | bytes 393220

commit v6 on v5

--- a/solution.py
+++ b/solution.py
@@ -56,36 +56,61 @@
     count = [0]
     batches = []
 
+    chips = NT // 2
+    has_up, has_down = s > 0, s < NS - 1
+    has1, has2 = chip >= 1, chip >= 2
+    has_far = chip >= 4 - core
+    to1, to2 = chip < chips - 1, chip < chips - 2
+    to_far = chip < chips - 3 - core
+
     def shift(by):
         return lax.rem(t + by + NT, NT)
 
-    def remote(src, dst, tm, sp):
+    def remote(src, dst, tm, sp, sends=None, receives=None):
         i = count[0]
         count[0] += 1
-        return pltpu.make_async_remote_copy(
+        copy = pltpu.make_async_remote_copy(
             src_ref=src, dst_ref=dst, send_sem=send.at[i], recv_sem=recv.at[i],
             device_id=(tm, sp), device_id_type=MESH,
         )
-
-    def batch(copies, given=None):
-        batches.append((copies, given))
-        when(given, lambda: [c.start() for c in copies])
-        return copies
+        return copy, sends, receives
+
+    def upward(src, dst, tm=t):
+        return remote(src, dst, tm, up, has_up, has_down)
+
+    def downward(src, dst, tm=t):
+        return remote(src, dst, tm, down, has_down, has_up)
 
     def when(given, act):
         if given is None:
             act()
         else:
-            pl.when(given)(lambda: (act(), None)[1])
-
-    def arrive(copies, given=None):
-        when(given, lambda: [c.wait_recv() for c in copies])
-
-    chips = NT // 2
-    has1, has2 = chip >= 1, chip >= 2
-    has_far = chip >= 4 - core
-    to1, to2 = chip < chips - 1, chip < chips - 2
-    to_far = chip < chips - 3 - core
+
+            @pl.when(given)
+            def _():
+                act()
+
+    def each(copies, which, act):
+        groups = []
+        for c in copies:
+            same = [g for g in groups if g[0] is c[which]]
+            if same:
+                same[0][1].append(c[0])
+            else:
+                groups.append((c[which], [c[0]]))
+        for given, members in groups:
+            when(given, lambda: [act(c) for c in members])
+
+    def begin(copies):
+        each(copies, 1, lambda c: c.start())
+
+    def batch(copies):
+        batches.append(copies)
+        begin(copies)
+        return copies
+
+    def arrive(copies):
+        each(copies, 2, lambda c: c.wait_recv())
 
     barrier = pltpu.get_barrier_semaphore()
 
@@ -95,8 +120,9 @@
     when(has_far, lambda: greet(shift(-7), s))
     when(has2, lambda: greet(shift(-4), s))
     when(has1, lambda: greet(shift(-2), s))
-    for tm, sp in ((mate, up), (mate, down), (t, up), (t, down), (mate, s)):
-        greet(tm, sp)
+    when(has_up, lambda: [greet(tm, up) for tm in (mate, t)])
+    when(has_down, lambda: [greet(tm, down) for tm in (mate, t)])
+    greet(mate, s)
 
     loads = [
         pltpu.make_async_copy(perm, k_buf.at[0:ROWS], local.at[0]),
@@ -111,36 +137,49 @@
     hz[3:5] = jnp.zeros((2, COLS), jnp.float32)
     cw[:, 5:11] = jnp.zeros((2, 6, HALF), jnp.float32)
 
-    @pl.when(jnp.logical_not(has1))
-    def _():
-        m1_in[...] = jnp.zeros_like(m1_in)
-
-    @pl.when(jnp.logical_not(has2))
-    def _():
-        m2_in[...] = jnp.zeros_like(m2_in)
-
-    @pl.when(jnp.logical_not(has_far))
-    def _():
-        far_in[...] = jnp.zeros_like(far_in)
+    def clear(ref):
+        ref[...] = jnp.zeros(ref.shape, jnp.float32)
+
+    when(jnp.logical_not(has1), lambda: clear(m1_in))
+    when(jnp.logical_not(has2), lambda: clear(m2_in))
+    when(jnp.logical_not(has_far), lambda: clear(far_in))
+
+    @pl.when(s == 0)
+    def _():
+        for ref in (
+            k_buf.at[24:32], cpg.at[0], cu.at[0:8], cb.at[:, 0:8], cz.at[0:8], hz, cw.at[:, 0:5], hw.at[:, 4:8]
+        ):
+            clear(ref)
+
+    @pl.when(s == NS - 1)
+    def _():
+        for ref in (
+            k_buf.at[16:24], cpg.at[1], cu.at[8:16], cb.at[:, 8:16], cz.at[8:16], hz, cw.at[:, 11:16], hw.at[:, 0:4]
+        ):
+            clear(ref)
+
+    def number(given, times=1):
+        return jnp.where(given, times, 0).astype(jnp.int32)
 
     pl.semaphore_wait(
-        barrier, 5 + to1.astype(jnp.int32) + to2.astype(jnp.int32) + to_far.astype(jnp.int32)
+        barrier,
+        1 + number(has_up, 2) + number(has_down, 2) + number(to1) + number(to2) + number(to_far),
     )
 
     k_halo = batch([
-        remote(perm.at[0:8], k_buf.at[16:24], t, up),
-        remote(perm.at[8:16], k_buf.at[24:32], t, down),
+        upward(perm.at[0:8], k_buf.at[16:24]),
+        downward(perm.at[8:16], k_buf.at[24:32]),
     ])
     for c in loads:
         c.wait()
     g_buf[...] = f_buf[0] - i_buf[0]
-    far = [remote(far_src, far_in, shift(7), s)]
-    batches.append((far, to_far))
+    far = [remote(far_src, far_in, shift(7), s, to_far, has_far)]
+    batches.append(far)
 
     @pl.when(jnp.logical_and(core == 0, to_far))
     def _():
         far_src[...] = g_buf[...]
-        far[0].start()
+        far[0][0].start()
 
     arrive(k_halo)
 
@@ -187,8 +226,8 @@
 
     pg[...] = apply(extend(g_buf[...], 24), w_mid)
     pg_halo = batch([
-        remote(pg.at[16:17], cpg.at[0], t, down),
-        remote(pg.at[23:24], cpg.at[1], t, up),
+        downward(pg.at[16:17], cpg.at[0]),
+        upward(pg.at[23:24], cpg.at[1]),
     ])
 
     for j in (1, 2, 3, 4):
@@ -206,14 +245,14 @@
     b_buf[2] = apply(b_buf[1], w_wide) + widen(r_buf[2])
     u_buf[...] = apply(b_buf[2], w_wide) + widen(r_buf[3])
     u_rim = batch([
-        remote(u_buf.at[16:24], cu.at[0:8], t, down),
-        remote(u_buf.at[24:32], cu.at[8:16], t, up),
+        downward(u_buf.at[16:24], cu.at[0:8]),
+        upward(u_buf.at[24:32], cu.at[8:16]),
     ])
     b_rim = []
     for j in range(3):
         b_rim += batch([
-            remote(b_buf.at[j, 16:24], cb.at[j, 0:8], t, down),
-            remote(b_buf.at[j, 24:32], cb.at[j, 8:16], t, up),
+            downward(b_buf.at[j, 16:24], cb.at[j, 0:8]),
+            upward(b_buf.at[j, 24:32], cb.at[j, 8:16]),
         ])
     arrive(pg_halo)
     pg[0:1] = pg[0:1] + cpg[0]
@@ -227,7 +266,7 @@
     @pl.when(jnp.logical_and(core == 1, to_far))
     def _():
         far_src[...] = u
-        far[0].start()
+        far[0][0].start()
 
     arrive(y_swap)
 
@@ -235,18 +274,18 @@
     window = pl.ds(start, WIN)
     yw[...] = apply(extend(y_buf[0, :, window], 24), w_mid, start) + extend(y_buf[1, :, window], 24)
     m1_copies = batch([
-        remote(yw.at[0:ROWS], m1_in.at[0:ROWS], shift(2), s),
-        remote(yw.at[16:17], m1_in.at[16:17], shift(2), s),
-        remote(yw.at[23:24], m1_in.at[23:24], shift(2), s),
-    ], to1)
+        remote(yw.at[0:ROWS], m1_in.at[0:ROWS], shift(2), s, to1, has1),
+        remote(yw.at[16:17], m1_in.at[16:17], shift(2), s, to1, has1),
+        remote(yw.at[23:24], m1_in.at[23:24], shift(2), s, to1, has1),
+    ])
 
     z_rim = [
-        remote(z_buf.at[16:24], cz.at[0:8], t, down),
-        remote(z_buf.at[24:32], cz.at[8:16], t, up),
-        remote(z_buf.at[0:3], hz.at[0:3], t, up),
-        remote(z_buf.at[13:16], hz.at[5:8], t, down),
+        downward(z_buf.at[16:24], cz.at[0:8]),
+        upward(z_buf.at[24:32], cz.at[8:16]),
+        upward(z_buf.at[0:3], hz.at[0:3]),
+        downward(z_buf.at[13:16], hz.at[5:8]),
     ]
-    batches.append((z_rim, None))
+    batches.append(z_rim)
 
     def far_term(more):
         v = extend(far_in[...], 24)
@@ -259,19 +298,18 @@
 
     @pl.when(core == 1)
     def _():
-        arrive(far, has_far)
+        arrive(far)
         z_buf[...] = extend(g_buf[...] + y_buf[0], 32) - far_term(3)
-        for c in z_rim:
-            c.start()
-
-
-    arrive(m1_copies, has1)
+        begin(z_rim)
+
+
+    arrive(m1_copies)
     m2[...] = apply(apply(m1_in[...], w_mid, start), w_mid, start) + yw[...]
     m2_copies = batch([
-        remote(m2.at[0:ROWS], m2_in.at[0:ROWS], shift(4), s),
-        remote(m2.at[16:19], m2_in.at[16:19], shift(4), s),
-        remote(m2.at[21:24], m2_in.at[21:24], shift(4), s),
-    ], to2)
+        remote(m2.at[0:ROWS], m2_in.at[0:ROWS], shift(4), s, to2, has2),
+        remote(m2.at[16:19], m2_in.at[16:19], shift(4), s, to2, has2),
+        remote(m2.at[21:24], m2_in.at[21:24], shift(4), s, to2, has2),
+    ])
 
     arrive(b_rim)
     for j in range(3):
@@ -279,12 +317,11 @@
 
     @pl.when(core == 0)
     def _():
-        arrive(far, has_far)
+        arrive(far)
         z_buf[...] = extend(g_buf[...], 32) + far_term(2)
-        for c in z_rim:
-            c.start()
-
-    arrive(m2_copies, has2)
+        begin(z_rim)
+
+    arrive(m2_copies)
     wide = apply(apply(widen(m2_in[...]), w_wide, start), w_wide, start)
     wide = widen(m1_in[...]) + wide
 
@@ -300,10 +337,10 @@
     w_rim = []
     for tm in (t, mate):
         w_rim += [
-            remote(mine.at[16:21], cw.at[core, 0:5], tm, down),
-            remote(mine.at[27:32], cw.at[core, 11:16], tm, up),
-            remote(mine.at[0:4], hw.at[core, 0:4], tm, up),
-            remote(mine.at[12:16], hw.at[core, 4:8], tm, down),
+            downward(mine.at[16:21], cw.at[core, 0:5], tm),
+            upward(mine.at[27:32], cw.at[core, 11:16], tm),
+            upward(mine.at[0:4], hw.at[core, 0:4], tm),
+            downward(mine.at[12:16], hw.at[core, 4:8], tm),
         ]
     w_rim = batch(w_rim)
     w_swap = batch([remote(mine, mine, mate, s)])
@@ -337,8 +374,8 @@
     for j in (1, 2, 3):
         state = apply(state, w_mid)
         out[j] = base[j - 1] + state[0:ROWS]
-    for copies, given in batches:
-        when(given, lambda: [c.wait_send() for c in copies])
+    for copies in batches:
+        each(copies, 1, lambda c: c.wait_send())
 
 
 def per_device(forcing, iterate, permeability):
@@ -384,14 +421,14 @@
     return pl.pallas_call(
         kernel,
         name="vcycle",
-        out_shape=jax.ShapeDtypeStruct(iterate.shape, iterate.dtype),
+        out_shape=pltpu.VMEM(iterate.shape, iterate.dtype),
         in_specs=[pl.BlockSpec(memory_space=pltpu.HBM)] * 3,
         out_specs=pl.BlockSpec(memory_space=pltpu.VMEM),
         scratch_shapes=scratch,
         compiler_params=pltpu.CompilerParams(
-            collective_id=0, has_side_effects=True, vmem_limit_bytes=int(53.25 * 2**20)
+            collective_id=0, has_side_effects=True, vmem_limit_bytes=24 * 2**20
         ),
-    )(forcing, iterate, permeability)
+    )(*(pltpu.with_memory_space_constraint(v, pltpu.HBM) for v in (forcing, iterate, permeability)))
 
 
 def solution(mesh):

time: 44.7 us -> 42.1 us (0.942)
  Pallas kernels: 42.9 us -> 41.1 us
  local copies, waits for them, and re-layouts: 1.7 us -> 0.8 us
    pallas_call x1, Pallas kernels: 42.9 us -> 41.1 us  [per_device(): pl.pallas_call(kernel, name='vcycle', out_shape=pltpu.VMEM(iterate.shape,...]
    unnamed x3 -> x1, local copies, waits for them, and re-layouts: 1.7 us -> 0.8 us
where the time goes in v6:
time: 42.1 us; the launch traced here: 41.9 us
  Pallas kernels  41.1 us (98%)
  local copies, waits for them, and re-layouts  0.8 us (2%)
    pallas_call x1, Pallas kernels, per_device(): pl.pallas_call(kernel, name='vcycle', out_shape=pltpu.VMEM(iterate.shape,...  41.1 us

profile of v6, /device:TPU:7, one launch (start us, length us, event | category | flops | bytes accessed | tf_op | source)
XLA Modules:
  0.0 41.9 jit_solution(7652876679439659844)
XLA Ops:
  0.0 41.1 %vcycle.1 = f32[4,16,2048]{2,1,0:T(8,128)S(1)} custom-call(f32[16,16,2048]{2,1,0:T(8,128)} %forcing.1, f32[4,16,2048]{2,1,0:T(8,128)} %iterate.1, f32[16,2048]{1,0:T(8,128)} %perm.1), custom_call_target="tpu_custom_call" | custom-call | tf_op jit(solution)/shard_map/vcycle/pallas_call | solution.py:421
  41.1 0.8 %copy.5 = f32[4,16,2048]{2,1,0:T(8,128)} copy(f32[4,16,2048]{2,1,0:T(8,128)S(1)} %vcycle.1) | data formatting | bytes 1048576

commit v7 on v6

--- a/solution.py
+++ b/solution.py
@@ -42,7 +42,7 @@
 
 def kernel(
     forcing, iterate, perm, out,
-    f_buf, i_buf, k_buf, w_fine, w_mid, w_wide, s_buf, r_buf, b_buf, g_buf, pg, u_buf, cu, cb, cpg, far_src, far_in,
+    f_buf, i_buf, k_buf, k_near_buf, w_fine, w_mid, w_wide, s_buf, r_buf, b_buf, g_buf, pg, u_buf, cu, cb, cpg, far_src, far_in,
     y_buf, yw, m1_in, m2, m2_in, z_buf, cz, hz, za, w_buf, cw, hw, w_sum, base,
     send, recv, local,
 ):
@@ -147,14 +147,14 @@
     @pl.when(s == 0)
     def _():
         for ref in (
-            k_buf.at[24:32], cpg.at[0], cu.at[0:8], cb.at[:, 0:8], cz.at[0:8], hz, cw.at[:, 0:5], hw.at[:, 4:8]
+            k_buf.at[24:32], k_near_buf.at[4:8], cpg.at[0], cu.at[0:8], cb.at[:, 0:8], cz.at[0:8], hz, cw.at[:, 0:5], hw.at[:, 4:8]
         ):
             clear(ref)
 
     @pl.when(s == NS - 1)
     def _():
         for ref in (
-            k_buf.at[16:24], cpg.at[1], cu.at[8:16], cb.at[:, 8:16], cz.at[8:16], hz, cw.at[:, 11:16], hw.at[:, 0:4]
+            k_buf.at[16:24], k_near_buf.at[0:4], cpg.at[1], cu.at[8:16], cb.at[:, 8:16], cz.at[8:16], hz, cw.at[:, 11:16], hw.at[:, 0:4]
         ):
             clear(ref)
 
@@ -166,7 +166,11 @@
         1 + number(has_up, 2) + number(has_down, 2) + number(to1) + number(to2) + number(to_far),
     )
 
-    k_halo = batch([
+    k_near = batch([
+        upward(perm.at[0:4], k_near_buf.at[0:4]),
+        downward(perm.at[12:16], k_near_buf.at[4:8]),
+    ])
+    k_far = batch([
         upward(perm.at[0:8], k_buf.at[16:24]),
         downward(perm.at[8:16], k_buf.at[24:32]),
     ])
@@ -181,48 +185,74 @@
         far_src[...] = g_buf[...]
         far[0][0].start()
 
-    arrive(k_halo)
-
-    row = lax.broadcasted_iota(jnp.int32, (32, 128), 0)
-    is_below = jnp.logical_and(row >= ROWS, row < ROWS + 8)
-    is_above = row >= ROWS + 8
-    outside = jnp.logical_or(
-        jnp.logical_and(is_below, s == NS - 1), jnp.logical_and(is_above, s == 0)
-    )
-    inside = jnp.where(outside, 0.0, 1.0).astype(jnp.float32)
-    lane = lax.broadcasted_iota(jnp.int32, (32, 128), 1)
-    in_above = pltpu.roll(inside, 1, axis=0) * inside
-    in_below = pltpu.roll(inside, 31, axis=0) * inside
-    near = lax.broadcasted_iota(jnp.int32, (8, 128), 0) < 4
-
-    def narrow(v):
-        return jnp.concatenate([v[0:ROWS], jnp.where(near, v[16:24], v[24:32])], axis=0)
-
-    for j in range(COLS // 128):
+    lane = lax.broadcasted_iota(jnp.int32, (1, 128), 1)
+    tiles = COLS // 128
+
+    def sides(part, j):
+        k = part(j)
+        zero = jnp.zeros_like(k)
+        kl = pltpu.roll(part(j - 1), 1, axis=1) if j else zero
+        kr = pltpu.roll(part(j + 1), 127, axis=1) if j < tiles - 1 else zero
+        left = 0.5 * (k + jnp.where(lane == 0, kl, pltpu.roll(k, 1, axis=1)))
+        right = 0.5 * (k + jnp.where(lane == 127, kr, pltpu.roll(k, 127, axis=1)))
+        return k, left, right
+
+    def closed(left, right, j):
+        if j == 0:
+            left = jnp.where(lane == 0, 0.0, left)
+        if j == tiles - 1:
+            right = jnp.where(lane == 127, 0.0, right)
+        return left, right
+
+    own_row = lax.broadcasted_iota(jnp.int32, (ROWS, 128), 0)
+    for j in range(tiles):
         at = slice(128 * j, 128 * j + 128)
-        k = k_buf[:, at] * inside
-        zero = jnp.zeros_like(k)
-        kl = k_buf[:, 128 * j - 128 : 128 * j] * inside if j else zero
-        kr = k_buf[:, 128 * j + 128 : 128 * j + 256] * inside if j < COLS // 128 - 1 else zero
-        k_left = jnp.where(lane == 0, pltpu.roll(kl, 1, axis=1), pltpu.roll(k, 1, axis=1))
-        k_right = jnp.where(lane == 127, pltpu.roll(kr, 127, axis=1), pltpu.roll(k, 127, axis=1))
-        wa = 0.5 * (k + pltpu.roll(k, 1, axis=0))
-        wb = 0.5 * (k + pltpu.roll(k, 31, axis=0))
-        wl = 0.5 * (k + k_left)
-        wr = 0.5 * (k + k_right)
+        k, wl, wr = sides(lambda i: k_buf[0:ROWS, 128 * i : 128 * i + 128], j)
+        k_above = jnp.where(own_row == 0, 0.0, pltpu.roll(k, 1, axis=0))
+        k_below = jnp.where(own_row == ROWS - 1, 0.0, pltpu.roll(k, ROWS - 1, axis=0))
+        wa = 0.5 * (k + k_above)
+        wb = 0.5 * (k + k_below)
         total = (wa + wb) + (wl + wr)
-        wa = wa * in_above
-        wb = wb * in_below
-        if j == 0:
-            wl = jnp.where(lane == 0, 0.0, wl)
-        if j == COLS // 128 - 1:
-            wr = jnp.where(lane == 127, 0.0, wr)
-        for i, v in enumerate((total, wa, wb, wl, wr)):
-            fine = 1.0 - STEP * v if i == 0 else STEP * v
-            mid = 1.0 - 4.0 * STEP * v if i == 0 else 4.0 * STEP * v
-            w_fine[i, :, at] = narrow(fine)
-            w_mid[i, :, at] = narrow(mid)
-            w_wide[i, :, at] = mid
+        wl, wr = closed(wl, wr, j)
+        for ref, c in ((w_fine, STEP), (w_mid, 4.0 * STEP)):
+            ref[0, 0:ROWS, at] = 1.0 - c * total
+            ref[1, 0:ROWS, at] = c * wa
+            ref[2, 0:ROWS, at] = c * wb
+            ref[3, 0:ROWS, at] = c * wl
+            ref[4, 0:ROWS, at] = c * wr
+
+    rim_row = lax.broadcasted_iota(jnp.int32, (8, 128), 0)
+    low = jnp.where(s < NS - 1, 1.0, 0.0).astype(jnp.float32)
+    high = jnp.where(s > 0, 1.0, 0.0).astype(jnp.float32)
+
+    def rim_weights(part, j, inside, first_above, last_below):
+        k, wl, wr = sides(part, j)
+        wa = 0.5 * (k + jnp.where(rim_row == 0, first_above, pltpu.roll(k, 1, axis=0)))
+        wb = 0.5 * (k + jnp.where(rim_row == 7, last_below, pltpu.roll(k, 7, axis=0)))
+        total = (wa + wb) + (wl + wr)
+        wl, wr = closed(wl, wr, j)
+        return total, inside * wa, inside * wb, wl, wr
+
+    arrive(k_near)
+    near = rim_row < 4
+    inside = jnp.where(near, low, high)
+    for j in range(tiles):
+        at = slice(128 * j, 128 * j + 128)
+
+        def part(i):
+            return inside * k_near_buf[:, 128 * i : 128 * i + 128]
+
+        top, bottom = k_buf[0:1, at], k_buf[15:16, at]
+        rim = part(j)
+        weights = rim_weights(part, j, inside, bottom, top)
+        for ref, c in ((w_fine, STEP), (w_mid, 4.0 * STEP)):
+            ref[0, ROWS:24, at] = 1.0 - c * weights[0]
+            for i in (1, 2, 3, 4):
+                ref[i, ROWS:24, at] = c * weights[i]
+            ref[0, 0:1, at] = ref[0, 0:1, at] - (0.5 * c) * rim[7:8]
+            ref[1, 0:1, at] = (high * 0.5 * c) * (top + rim[7:8])
+            ref[0, 15:16, at] = ref[0, 15:16, at] - (0.5 * c) * rim[0:1]
+            ref[2, 15:16, at] = (low * 0.5 * c) * (bottom + rim[0:1])
 
     pg[...] = apply(extend(g_buf[...], 24), w_mid)
     pg_halo = batch([
@@ -239,6 +269,22 @@
                 r_buf[p] = state + extend(f_buf[4 * p + 4] - i_buf[p + 1], 24)
             else:
                 r_buf[3] = state
+
+    arrive(k_far)
+    for j in range(tiles):
+        at = slice(128 * j, 128 * j + 128)
+        for lo, inside in ((16, low), (24, high)):
+
+            def part(i):
+                return inside * k_buf[lo : lo + 8, 128 * i : 128 * i + 128]
+
+            above = k_buf[15:16, at] if lo == 16 else jnp.zeros((1, 128), jnp.float32)
+            below = k_buf[0:1, at] if lo == 24 else jnp.zeros((1, 128), jnp.float32)
+            weights = rim_weights(part, j, inside, above, below)
+            w_wide[0, lo : lo + 8, at] = 1.0 - (4.0 * STEP) * weights[0]
+            for i in (1, 2, 3, 4):
+                w_wide[i, lo : lo + 8, at] = (4.0 * STEP) * weights[i]
+    w_wide[:, 0:ROWS] = w_mid[:, 0:ROWS]
 
     b_buf[0] = widen(r_buf[0])
     b_buf[1] = apply(b_buf[0], w_wide) + widen(r_buf[1])
@@ -386,6 +432,7 @@
         field(16, ROWS, COLS),
         field(4, ROWS, COLS),
         field(32, COLS),
+        field(8, COLS),
         field(5, 24, COLS),
         field(5, 24, COLS),
         field(5, 32, COLS),

time: 42.1 us -> 39.5 us (0.938)
  the two profiles are of different devices: /device:TPU:7 before, /device:TPU:39 now
where the time goes in v7:
time: 39.5 us; the launch traced here: 39.3 us
  Pallas kernels  38.5 us (97%)
  local copies, waits for them, and re-layouts  0.8 us (2%)
    pallas_call x1, Pallas kernels, per_device(): pl.pallas_call(kernel, name='vcycle', out_shape=pltpu.VMEM(iterate.shape,...  38.5 us
    unnamed x1, local copies, waits for them, and re-layouts  0.8 us

profile of v7, /device:TPU:39, one launch (start us, length us, event | category | flops | bytes accessed | tf_op | source)
XLA Modules:
  0.0 39.3 jit_solution(4768606477928811744)
XLA Ops:
  0.0 38.5 %vcycle.1 = f32[4,16,2048]{2,1,0:T(8,128)S(1)} custom-call(f32[16,16,2048]{2,1,0:T(8,128)} %forcing.1, f32[4,16,2048]{2,1,0:T(8,128)} %iterate.1, f32[16,2048]{1,0:T(8,128)} %perm.1), custom_call_target="tpu_custom_call" | custom-call | tf_op jit(solution)/shard_map/vcycle/pallas_call | solution.py:468
  38.6 0.8 %copy.5 = f32[4,16,2048]{2,1,0:T(8,128)} copy(f32[4,16,2048]{2,1,0:T(8,128)S(1)} %vcycle.1) | data formatting | bytes 1048576
